TPU v7x, 128 devices: a whole 4x4x4 slice. The times are simulated.
128 devices in a mesh: dp: 16 (over x, z), seq: 8 (over y, core).
Axes of the slice: x: 4, y: 4, z: 4, core: 2. Of those that a mesh axis runs over, the one named last changes fastest.
Arguments:
- hidden: bfloat16 [16384, 4096], P(('dp', 'seq')), may hold values from -6 to 6
- w_query: bfloat16 [4096, 2048], P('dp'), may hold values from -0.09375 to 0.09375
- nbr_keys: bfloat16 [512, 128, 2048], P(('dp', 'seq')), may hold values from -50 to 50
- nbr_values: bfloat16 [512, 128, 2048], P(('dp', 'seq')), may hold values from -6 to 6
- nbr_ids: int32 [256, 2], P(('dp', 'seq')), may hold values from 0 to 31, as said below
- d_attended: bfloat16 [16384, 2048], P(('dp', 'seq')), may hold values from -6 to 6
Outputs:
- attended: bfloat16 [16384, 2048], P(('dp', 'seq'))
- d_hidden: bfloat16 [16384, 4096], P(('dp', 'seq'))
- d_wq: float32 [4096, 2048], P('seq', 'dp')
- d_keys: float32 [512, 128, 2048], P(('dp', 'seq'))
- d_values: float32 [512, 128, 2048], P(('dp', 'seq'))
Inputs may be any that keep to these rules, and one draw needn't show every extreme that they name: `nbr_ids`: the 4 ids held by one device (2 blocks × 2 neighbours) are distinct and lie in 4 different seq shards of the group (the shard of an id is id // 4).
All inputs are finite; a program needn't handle non-finite values.
Results may differ from a plain program's by a relative error of at most 0.019.
The roundings to bfloat16 on the way count: a program that leaves them out, or rounds other values in their place, can miss the bound.
Values may be sent and summed in bfloat16 or wider, within the bound.
A program may use at most 128 MiB of HBM per device.

v0:
```python
import jax
import jax.numpy as jnp
from jax import lax
from jax.sharding import PartitionSpec as P

HEAD_DIM = 128


def on_device(hidden, w_query, nbr_keys, nbr_values, nbr_ids, d_attended):
    tokens_here, width = hidden.shape
    blocks_here, neigh_count = nbr_ids.shape
    held_rows, neigh_len, query_width = nbr_keys.shape
    shards = lax.axis_size("seq")
    requests = neigh_count * blocks_here
    capacity = (requests + shards - 1) // shards
    block_len = tokens_here // blocks_here
    head_count = query_width // HEAD_DIM
    scale = HEAD_DIM ** (-0.5)
    whole_weight = lax.all_gather(w_query, "dp", axis=0, tiled=True)
    query = jnp.dot(hidden, whole_weight, preferred_element_type=jnp.float32).astype(jnp.bfloat16)
    wanted = nbr_ids.reshape(-1)
    owner = wanted // held_rows
    local_row = wanted % held_rows
    owner_hits = (owner[:, None] == jnp.arange(shards, dtype=jnp.int32)[None, :]).astype(jnp.int32)
    earlier = jnp.cumsum(owner_hits, axis=0) - owner_hits
    rank = jnp.sum(earlier * owner_hits, axis=1)
    slot_index = owner * capacity + rank
    slot_range = jnp.arange(shards * capacity, dtype=jnp.int32)
    slot_match = slot_index[None, :] == slot_range[:, None]
    table = jnp.sum(jnp.where(slot_match, local_row[None, :] + 1, 0), axis=1) - 1
    asked = lax.all_to_all(
        table.reshape(shards, capacity), "seq", split_axis=0, concat_axis=0, tiled=True
    )
    asked_flat = asked.reshape(-1)
    safe_rows = jnp.clip(asked_flat, 0, held_rows - 1)
    send_keys = jnp.take(nbr_keys, safe_rows, axis=0).reshape(
        shards, capacity, neigh_len, query_width
    )
    send_values = jnp.take(nbr_values, safe_rows, axis=0).reshape(
        shards, capacity, neigh_len, query_width
    )
    got_keys, got_values = (
        lax.all_to_all(send_keys, "seq", split_axis=0, concat_axis=0, tiled=True),
        lax.all_to_all(send_values, "seq", split_axis=0, concat_axis=0, tiled=True),
    )
    keys = jnp.take(got_keys.reshape(shards * capacity, neigh_len, query_width), slot_index, axis=0)
    values = jnp.take(
        got_values.reshape(shards * capacity, neigh_len, query_width), slot_index, axis=0
    )
    keys = keys.reshape(blocks_here, neigh_count * neigh_len, head_count, HEAD_DIM)
    values = values.reshape(blocks_here, neigh_count * neigh_len, head_count, HEAD_DIM)
    queries = query.reshape(blocks_here, block_len, head_count, HEAD_DIM)
    scores = (
        jnp.einsum("cqhd,ckhd->chqk", queries, keys, preferred_element_type=jnp.float32) * scale
    )
    peak = jnp.max(scores, axis=-1, keepdims=True)
    expo = jnp.exp(scores - peak)
    probs = expo / jnp.sum(expo, axis=-1, keepdims=True)
    probs_low = probs.astype(jnp.bfloat16)
    attended = jnp.einsum("chqk,ckhd->cqhd", probs_low, values, preferred_element_type=jnp.float32)
    attended = attended.astype(jnp.bfloat16).reshape(tokens_here, query_width)
    grads = d_attended.reshape(blocks_here, block_len, head_count, HEAD_DIM)
    d_probs = jnp.einsum("cqhd,ckhd->chqk", grads, values, preferred_element_type=jnp.float32)
    delta = jnp.sum(probs * d_probs, axis=-1, keepdims=True)
    d_scores = (probs * (d_probs - delta) * scale).astype(jnp.bfloat16)
    d_query = jnp.einsum("chqk,ckhd->cqhd", d_scores, keys, preferred_element_type=jnp.float32)
    d_query = d_query.astype(jnp.bfloat16).reshape(tokens_here, query_width)
    key_parts = jnp.einsum(
        "chqk,cqhd->ckhd", d_scores, queries, preferred_element_type=jnp.float32
    ).astype(jnp.bfloat16)
    value_parts = jnp.einsum(
        "chqk,cqhd->ckhd", probs_low, grads, preferred_element_type=jnp.float32
    ).astype(jnp.bfloat16)
    placing = slot_match.astype(jnp.bfloat16)
    back_keys = jnp.dot(
        placing, key_parts.reshape(requests, -1), preferred_element_type=jnp.float32
    )
    back_values = jnp.dot(
        placing, value_parts.reshape(requests, -1), preferred_element_type=jnp.float32
    )
    back_keys = back_keys.astype(jnp.bfloat16).reshape(shards, capacity, neigh_len, query_width)
    back_values = back_values.astype(jnp.bfloat16).reshape(shards, capacity, neigh_len, query_width)
    ret_keys, ret_values = (
        lax.all_to_all(back_keys, "seq", split_axis=0, concat_axis=0, tiled=True),
        lax.all_to_all(back_values, "seq", split_axis=0, concat_axis=0, tiled=True),
    )
    collect = (asked_flat[None, :] == jnp.arange(held_rows, dtype=jnp.int32)[:, None]).astype(
        jnp.bfloat16
    )
    d_keys = jnp.dot(
        collect, ret_keys.reshape(shards * capacity, -1), preferred_element_type=jnp.float32
    )
    d_values = jnp.dot(
        collect, ret_values.reshape(shards * capacity, -1), preferred_element_type=jnp.float32
    )
    d_keys = d_keys.reshape(held_rows, neigh_len, query_width)
    d_values = d_values.reshape(held_rows, neigh_len, query_width)
    d_hidden = lax.dot_general(
        d_query, whole_weight, (((1,), (1,)), ((), ())), preferred_element_type=jnp.float32
    ).astype(jnp.bfloat16)
    feature_slice = lax.all_to_all(hidden, "seq", split_axis=1, concat_axis=0, tiled=True)
    group_grads = lax.all_gather(d_query, "seq", axis=0, tiled=True)
    partial_value = lax.dot_general(
        feature_slice, group_grads, (((0,), (0,)), ((), ())), preferred_element_type=jnp.float32
    )
    d_wq = lax.psum_scatter(partial_value, "dp", scatter_dimension=1, tiled=True)
    return (attended, d_hidden, d_wq, d_keys, d_values)


def solution(mesh):
    placed = (
        P(("dp", "seq"), None),
        P("dp", None),
        P(("dp", "seq"), None, None),
        P(("dp", "seq"), None, None),
        P(("dp", "seq"), None),
        P(("dp", "seq"), None),
    )
    return jax.shard_map(
        on_device,
        mesh=mesh,
        in_specs=placed,
        out_specs=(
            P(("dp", "seq"), None),
            P(("dp", "seq"), None),
            P("seq", "dp"),
            P(("dp", "seq"), None, None),
            P(("dp", "seq"), None, None),
        ),
        check_vma=False,
    )
```

profile of v0, /device:TPU:1, one launch (start us, length us, event | category | flops | bytes accessed | tf_op | source)
XLA Modules:
  0.0 384.3 jit_solution(9876784510760668222)
XLA Ops:
  7.2 0.7 all-gather.3.cloned.1.call-update
  7.9 0.8 reshape.182
  9.2 10.3 %all_to_all.45 = s32[8,1,1]{2,1,0:T(1,128)S(1)} all-to-all(s32[8,1,1]{2,1,0:T(1,128)S(1)} %copy.94), channel_id=1, replica_groups=mesh['dp'=16,'seq'=8] {'seq'}, dimensions={0} | all-to-all | bytes 64 | tf_op jit(solution)/shard_map/all_to_all | solution.py:31
  19.8 2.8 gather_fusion.2
  22.6 4.7 %gather_fusion = bf16[8,128,2048]{2,1,0:T(8,128)(2,1)} fusion(bf16[4,128,2048]{2,1,0:T(8,128)(2,1)} %param.13, s32[1024]{0:T(1024)S(1)} %pad_clamp_fusion.1), kind=kCustom, calls=%fused_computation.clone | custom fusion | bytes 8388640 | tf_op jit(solution)/shard_map/jit(_take)/gather | solution.py:39
  27.3 6.3 %select_bitcast_fusion = (bf16[8,1,128,2048]{3,2,1,0:T(8,128)(2,1)S(1)}, bf16[8,1,128,2048]{3,2,1,0:T(8,128)(2,1)}) fusion(bf16[8,128,2048]{2,1,0:T(8,128)(2,1)} %gather_fusion.2, pred[8]{0:T(512)(128)(4,1)S(1)} %get-tuple-element.39, bf16[8,128,2048]{2,1,0:T(8,128)(2,1)} %gather_fusion), kind=kLoop, calls=%fused_computation.9 | loop fusion | flops 4194304 | bytes 16777224 | tf_op jit(solution)/shard_map/reshape | solution.py:36
  33.6 53.2 %all_to_all.46 = bf16[8,1,128,2048]{3,2,1,0:T(8,128)(2,1)} all-to-all(bf16[8,1,128,2048]{3,2,1,0:T(8,128)(2,1)S(1)} %get-tuple-element.43), channel_id=1, replica_groups=mesh['dp'=16,'seq'=8] {'seq'}, dimensions={0} | all-to-all | bytes 8388608 | tf_op jit(solution)/shard_map/all_to_all | solution.py:43
  86.8 5.6 %all-to-all-start.1 = ((bf16[8,1,128,2048]{3,2,1,0:T(8,128)(2,1)}), bf16[8,1,128,2048]{3,2,1,0:T(8,128)(2,1)}, u32[]{:S(2)}, u32[]{:S(2)}) async-start(bf16[8,1,128,2048]{3,2,1,0:T(8,128)(2,1)} %get-tuple-element.44), calls=%async_computation.1 | async-start | bytes 8388608 | tf_op jit(solution)/shard_map/all_to_all | solution.py:44
  93.0 0.9 copy.118
  93.9 2.9 gather_fusion.3
  96.8 44.6 %all-to-all-done.1 = bf16[8,1,128,2048]{3,2,1,0:T(8,128)(2,1)} async-done(((bf16[8,1,128,2048]{3,2,1,0:T(8,128)(2,1)}), bf16[8,1,128,2048]{3,2,1,0:T(8,128)(2,1)}, u32[]{:S(2)}, u32[]{:S(2)}) %all-to-all-start.1) | async-done | bytes 4194336 | tf_op jit(solution)/shard_map/all_to_all | solution.py:44
  141.4 4.2 %gather_fusion.1 = bf16[4,128,2048]{2,1,0:T(8,128)(2,1)} fusion(bf16[8,128,2048]{2,1,0:T(8,128)(2,1)} %bitcast.2, s32[1024]{0:T(1024)S(1)} %pad_clamp_fusion), kind=kCustom, calls=%fused_computation.1.clone | custom fusion | bytes 4194320 | tf_op jit(solution)/shard_map/jit(_take)/gather | solution.py:47
  145.6 2.0 broadcast_select_fusion
  147.6 0.6 copy.116
  148.2 2.0 copy.115
  150.2 2.2 fusion.6
  152.5 8.3 %fusion.20 = bf16[16,8,16,128]{3,1,2,0:T(8,128)(2,1)S(1)} fusion(bf16[128,4096]{1,0:T(8,128)(2,1)S(1)} %copy-done.6, bf16[4096,2048]{1,0:T(8,128)(2,1)} %all-gather.3.cloned.1.call-done), kind=kOutput, calls=%fused_computation.35 | convolution fusion | flops 2147745792 | bytes 18350080 | tf_op jit(solution)/shard_map/dot_general | solution.py:20
  160.9 0.8 fusion.12
  161.7 2.0 fusion.59
  163.7 15.4 %fusion.24 = bf16[2,64,16,128]{3,1,2,0:T(8,128)(2,1)S(1)} fusion(bf16[2,256,16,128]{3,2,1,0:T(8,128)(2,1)} %bitcast.106, f32[2,16,256,64]{2,3,1,0:T(8,128)} %fusion.6, f32[2,16,64,256]{3,2,1,0:T(8,128)} %get-tuple-element.48, f32[2,16,64]{2,1,0:T(8,128)S(1)} %get-tuple-element.47), kind=kOutput, calls=%fused_computation.37 | convolution fusion | flops 138152192 | bytes 6823936 | tf_op jit(solution)/shard_map/chqk,ckhd->cqhd/dot_general | solution.py:66
  179.5 1.0 copy.157
  180.5 1.3 copy.103
  181.8 25.7 %all_to_all.47 = bf16[128,8,512]{0,2,1:T(8,128)(2,1)S(1)} all-to-all(bf16[128,8,512]{0,2,1:T(8,128)(2,1)} %bitcast.113), channel_id=1, replica_groups=mesh['dp'=16,'seq'=8] {'seq'}, dimensions={1} | all-to-all | bytes 2097152 | tf_op jit(solution)/shard_map/all_to_all | solution.py:101
  208.0 12.2 %all-gather.5.cloned.1.call-done = bf16[1024,2048]{1,0:T(8,128)(2,1)} async-done(((bf16[128,2048]{1,0:T(8,128)(2,1)}), bf16[1024,2048]{1,0:T(8,128)(2,1)}) %all-gather.5.cloned.1.call-update) | async-done | bytes 4194320 | tf_op jit(solution)/shard_map/all_gather | solution.py:102
  220.3 6.5 %convolution_bitcast_fusion = f32[512,2048]{0,1:T(8,128)} fusion(bf16[1024,2048]{1,0:T(8,128)(2,1)} %all-gather.5.cloned.1.call-done, bf16[1024,512]{1,0:T(8,128)(2,1)S(1)} %bitcast.120), kind=kOutput, calls=%fused_computation.11 | convolution fusion | flops 2147483648 | bytes 9437184 | tf_op jit(solution)/shard_map/dot_general | solution.py:103
  226.8 1.0 copy-done.12
  227.8 16.5 %convert_bitcast_fusion.1 = bf16[2,256,16,128]{1,3,2,0:T(8,128)(2,1)} fusion(f32[2,16,256,64]{2,3,1,0:T(8,128)} %fusion.6, bf16[2,64,16,128]{3,2,1,0:T(8,128)(2,1)S(1)} %bitcast.117, f32[2,16,64,256]{3,2,1,0:T(8,128)} %get-tuple-element.48, f32[2,16,64]{2,1,0:T(8,128)S(1)} %get-tuple-element.47), kind=kOutput, calls=%fused_computation.19 | convolution fusion | flops 138938624 | bytes 6823936 | tf_op jit(solution)/shard_map/chqk,cqhd->ckhd/dot_general | solution.py:68
  244.3 4.5 %copy.106 = bf16[2,256,16,128]{3,2,1,0:T(8,128)(2,1)} copy(bf16[2,256,16,128]{1,3,2,0:T(8,128)(2,1)} %convert_bitcast_fusion.1) | data formatting | bytes 4194304 | tf_op jit(solution)/shard_map/convert_element_type | solution.py:70
  248.8 2.4 reshape.194
  251.2 1.9 convolution_convert_fusion.1
  253.1 4.3 %copy.107 = bf16[8,1,128,2048]{3,2,1,0:T(8,128)(2,1)} copy(bf16[8,1,128,2048]{3,0,2,1:T(8,128)(2,1)S(1)} %bitcast.102) | data formatting | bytes 8388608 | tf_op jit(solution)/shard_map/reshape | solution.py:81
  257.4 5.2 %all-to-all-start.4 = ((bf16[8,1,128,2048]{3,2,1,0:T(8,128)(2,1)}), bf16[8,1,128,2048]{3,2,1,0:T(8,128)(2,1)}, u32[]{:S(2)}, u32[]{:S(2)}) async-start(bf16[8,1,128,2048]{3,2,1,0:T(8,128)(2,1)} %copy.107), calls=%async_computation.5 | async-start | bytes 8388608 | tf_op jit(solution)/shard_map/all_to_all | solution.py:84
  262.6 7.3 %convert_bitcast_fusion = bf16[2,256,16,128]{3,1,2,0:T(8,128)(2,1)} fusion(bf16[2,64,16,128]{3,2,1,0:T(8,128)(2,1)S(1)} %bitcast.115, f32[2,16,64]{2,1,0:T(8,128)S(1)} %get-tuple-element.47, f32[2,16,64,256]{3,2,1,0:T(8,128)} %copy-done.4), kind=kOutput, calls=%fused_computation.18 | convolution fusion | flops 137365760 | bytes 4726784 | tf_op jit(solution)/shard_map/chqk,cqhd->ckhd/dot_general | solution.py:71
  269.9 4.3 %copy.109 = bf16[2,256,16,128]{3,2,1,0:T(8,128)(2,1)} copy(bf16[2,256,16,128]{3,1,2,0:T(8,128)(2,1)} %convert_bitcast_fusion) | data formatting | bytes 4194304 | tf_op jit(solution)/shard_map/convert_element_type | solution.py:73
  274.2 2.4 reshape.197
  276.6 1.9 convolution_convert_fusion
  278.4 4.2 %copy.110 = bf16[8,1,128,2048]{3,2,1,0:T(8,128)(2,1)} copy(bf16[8,1,128,2048]{3,0,2,1:T(8,128)(2,1)S(1)} %bitcast.101) | data formatting | bytes 8388608 | tf_op jit(solution)/shard_map/reshape | solution.py:82
  282.7 28.7 %all-to-all-done.4 = bf16[8,1,128,2048]{3,2,1,0:T(8,128)(2,1)} async-done(((bf16[8,1,128,2048]{3,2,1,0:T(8,128)(2,1)}), bf16[8,1,128,2048]{3,2,1,0:T(8,128)(2,1)}, u32[]{:S(2)}, u32[]{:S(2)}) %all-to-all-start.4) | async-done | bytes 4194336 | tf_op jit(solution)/shard_map/all_to_all | solution.py:84
  311.4 5.6 %all-to-all-start.5 = ((bf16[8,1,128,2048]{3,2,1,0:T(8,128)(2,1)}), bf16[8,1,128,2048]{3,2,1,0:T(8,128)(2,1)}, u32[]{:S(2)}, u32[]{:S(2)}) async-start(bf16[8,1,128,2048]{3,2,1,0:T(8,128)(2,1)} %copy.110), calls=%async_computation.6 | async-start | bytes 8388608 | tf_op jit(solution)/shard_map/all_to_all | solution.py:85
  317.0 5.3 %fusion.21 = bf16[2,64,16,128]{3,1,2,0:T(8,128)(2,1)S(1)} fusion(bf16[2,256,16,128]{3,2,1,0:T(8,128)(2,1)S(1)} %bitcast.105, f32[2,16,64]{2,1,0:T(8,128)S(1)} %get-tuple-element.47, f32[2,16,64,256]{3,2,1,0:T(8,128)} %copy-done.4), kind=kOutput, calls=%fused_computation.36 | convolution fusion | flops 136579328 | bytes 4726784 | tf_op jit(solution)/shard_map/chqk,ckhd->cqhd/dot_general | solution.py:60
  322.6 0.9 copy.158
  323.6 12.4 %convolution_convert_fusion.2 = bf16[128,4096]{1,0:T(8,128)(2,1)} fusion(bf16[4096,2048]{1,0:T(8,128)(2,1)} %all-gather.3.cloned.1.call-done, bf16[16,8,16,128]{3,2,1,0:T(8,128)(2,1)S(1)} %bitcast.111), kind=kOutput, calls=%fused_computation.8 | convolution fusion | flops 2148007936 | bytes 18350080 | tf_op jit(solution)/shard_map/dot_general | solution.py:98
  335.9 5.3 %fusion.39 = f32[4,128,2048]{2,0,1:T(4,128)S(1)} fusion(s32[8]{0:T(128)S(1)} %reduce, bf16[1,8,128,2048]{3,2,1,0:T(8,128)(2,1)} %bitcast.45), kind=kOutput, calls=%fused_computation.65 | convolution fusion | flops 16777248 | bytes 8388640 | tf_op jit(solution)/shard_map/dot_general | solution.py:90
  341.2 4.7 %copy.112 = f32[4,128,2048]{2,1,0:T(8,128)} copy(f32[4,128,2048]{2,0,1:T(4,128)S(1)} %fusion.39) | data formatting | bytes 8388608
  346.0 19.7 %all-to-all-done.5 = bf16[8,1,128,2048]{3,2,1,0:T(8,128)(2,1)} async-done(((bf16[8,1,128,2048]{3,2,1,0:T(8,128)(2,1)}), bf16[8,1,128,2048]{3,2,1,0:T(8,128)(2,1)}, u32[]{:S(2)}, u32[]{:S(2)}) %all-to-all-start.5) | async-done | bytes 4194336 | tf_op jit(solution)/shard_map/all_to_all | solution.py:85
  365.7 5.3 %fusion.37 = f32[4,128,2048]{2,0,1:T(4,128)S(1)} fusion(s32[8]{0:T(128)S(1)} %reduce, bf16[1,8,128,2048]{3,2,1,0:T(8,128)(2,1)} %bitcast.49), kind=kOutput, calls=%fused_computation.64 | convolution fusion | flops 16777248 | bytes 8388640 | tf_op jit(solution)/shard_map/dot_general | solution.py:93
  371.0 4.4 %copy.113 = f32[4,128,2048]{2,1,0:T(8,128)} copy(f32[4,128,2048]{2,0,1:T(4,128)S(1)} %fusion.37) | data formatting | bytes 8388608
  375.4 1.8 copy.111
  (51 shorter events, 2.8 us)
Async XLA Ops:
  7.2 12.6 %copy-start = (bf16[4,128,2048]{2,1,0:T(8,128)(2,1)S(1)}, bf16[4,128,2048]{2,1,0:T(8,128)(2,1)}, u32[]{:S(2)}) copy-start(bf16[4,128,2048]{2,1,0:T(8,128)(2,1)} %param.12) | copy-start | bytes 6291460
  7.2 145.3 %all-gather.3.cloned.1.call-start = ((), (), s32[]{:S(2)}) async-start(), calls=%async_computation.7 | async-start | bytes 17825792 | tf_op jit(solution)/shard_map/all_gather | solution.py:19
  86.8 6.1 %copy-start.13 = (bf16[128,2048]{1,0:T(8,128)(2,1)S(1)}, bf16[128,2048]{1,0:T(8,128)(2,1)}, u32[]{:S(2)}) copy-start(bf16[128,2048]{1,0:T(8,128)(2,1)} %param.15) | copy-start | bytes 1572868
  86.8 54.5 %all-to-all-start.1 = ((bf16[8,1,128,2048]{3,2,1,0:T(8,128)(2,1)}), bf16[8,1,128,2048]{3,2,1,0:T(8,128)(2,1)}, u32[]{:S(2)}, u32[]{:S(2)}) async-start(bf16[8,1,128,2048]{3,2,1,0:T(8,128)(2,1)} %get-tuple-element.44), calls=%async_computation.1 | async-start | bytes 8388608 | tf_op jit(solution)/shard_map/all_to_all | solution.py:44
  92.4 127.8 %all-gather.5.cloned.1.call-start = ((), (), s32[]{:S(2)}) async-start(), calls=%async_computation.8 | async-start | bytes 4718592 | tf_op jit(solution)/shard_map/all_gather | solution.py:102
  148.2 2.0 copy-start.2
  148.2 2.0 copy-start.9
  150.2 2.2 copy-start.6
  152.5 8.4 %copy-start.5 = (bf16[64,8,16,128]{3,2,1,0:T(8,128)(2,1)S(1)}, bf16[64,8,16,128]{3,2,1,0:T(8,128)(2,1)}, u32[]{:S(2)}) copy-start(bf16[64,8,16,128]{3,2,1,0:T(8,128)(2,1)} %copy.115) | copy-start | bytes 6291460
  160.9 0.9 copy-start.11
  161.7 2.0 copy-start.4
  179.5 28.1 %copy-start.7 = (bf16[2,64,16,128]{3,2,1,0:T(8,128)(2,1)}, bf16[2,64,16,128]{3,2,1,0:T(8,128)(2,1)S(1)}, u32[]{:S(2)}) copy-start(bf16[2,64,16,128]{3,2,1,0:T(8,128)(2,1)S(1)} %copy.102) | copy-start | bytes 1572868
  180.4 195.0 %reduce-scatter.2.cloned.1.call-start = ((), (), s32[]{:S(2)}) async-start(), calls=%async_computation.9 | async-start | bytes 4456448 | tf_op jit(solution)/shard_map/reduce_scatter | solution.py:106
  226.8 1.0 copy-start.12
  257.4 5.2 %copy-start.10 = (bf16[16,8,16,128]{3,2,1,0:T(8,128)(2,1)S(1)}, bf16[16,8,16,128]{3,2,1,0:T(8,128)(2,1)}, u32[]{:S(2)}) copy-start(bf16[16,8,16,128]{3,2,1,0:T(8,128)(2,1)} %copy.118) | copy-start | bytes 1572868
  257.4 54.0 %all-to-all-start.4 = ((bf16[8,1,128,2048]{3,2,1,0:T(8,128)(2,1)}), bf16[8,1,128,2048]{3,2,1,0:T(8,128)(2,1)}, u32[]{:S(2)}, u32[]{:S(2)}) async-start(bf16[8,1,128,2048]{3,2,1,0:T(8,128)(2,1)} %copy.107), calls=%async_computation.5 | async-start | bytes 8388608 | tf_op jit(solution)/shard_map/all_to_all | solution.py:84
  282.7 34.3 %copy-start.3 = (bf16[64,8,16,128]{3,2,1,0:T(8,128)(2,1)S(1)}, bf16[64,8,16,128]{3,2,1,0:T(8,128)(2,1)}, u32[]{:S(2)}) copy-start(bf16[64,8,16,128]{3,2,1,0:T(8,128)(2,1)} %copy-done.2) | copy-start | bytes 6291460
  311.4 54.3 %all-to-all-start.5 = ((bf16[8,1,128,2048]{3,2,1,0:T(8,128)(2,1)}), bf16[8,1,128,2048]{3,2,1,0:T(8,128)(2,1)}, u32[]{:S(2)}, u32[]{:S(2)}) async-start(bf16[8,1,128,2048]{3,2,1,0:T(8,128)(2,1)} %copy.110), calls=%async_computation.6 | async-start | bytes 8388608 | tf_op jit(solution)/shard_map/all_to_all | solution.py:85
  322.3 1.3 copy-start.8
  371.0 6.2 %copy-start.1 = (bf16[4,128,2048]{2,1,0:T(8,128)(2,1)S(1)}, bf16[4,128,2048]{2,1,0:T(8,128)(2,1)}, u32[]{:S(2)}) copy-start(bf16[4,128,2048]{2,1,0:T(8,128)(2,1)} %param.12) | copy-start | bytes 6291460
Sparse Core Ops, SparseCore 0:
  10.2 114.6 all-gather.2
  180.6 39.6 all-gather.4
  226.9 76.9 reduce-scatter.1
where the time goes:
time: 388 us; the launch traced here: 384 us
  waiting for transfers between devices  106 us (27%)
  blocking collectives  89.3 us (23%)
  matrix products  89 us (23%)
  local copies, waits for them, and re-layouts  57.6 us (15%)
  starting transfers between devices  17 us (4%)
  between operations  14.5 us (4%)
  other arithmetic  11 us (3%)
    all_to_all x1, blocking collectives, on_device(): lax.all_to_all(send_keys, 'seq', split_axis=0, concat_axis=0, tiled=True)  53.2 us
    all_to_all x1, waiting for transfers between devices, on_device(): lax.all_to_all(send_values, 'seq', split_axis=0, concat_axis=0, tiled=True)  44.6 us
    all_to_all x1, waiting for transfers between devices, on_device(): lax.all_to_all(back_keys, 'seq', split_axis=0, concat_axis=0, tiled=True)  28.7 us
    all_to_all x1, blocking collectives, on_device(): lax.all_to_all(hidden, 'seq', split_axis=1, concat_axis=0, tiled=True)  25.7 us
    all_to_all x1, waiting for transfers between devices, on_device(): lax.all_to_all(back_values, 'seq', split_axis=0, concat_axis=0, tiled=True)  19.7 us
    unnamed x38, local copies, waits for them, and re-layouts  18.9 us
    dot_general x1, matrix products, on_device(): jnp.einsum('chqk,cqhd->ckhd', d_scores, queries, preferred_element_type=j...  16.5 us
    dot_general x1, matrix products, on_device(): jnp.einsum('chqk,ckhd->cqhd', d_scores, keys, preferred_element_type=jnp....  15.4 us
  transfers between devices with their start and end apart: 6, of which 4 were waited for; matrix products, arithmetic and copies ran while one was open for 31% of the time, Pallas kernels for 0%

commit v1 on v0

v1 whole, which is shorter than its diff:
```python
import functools

import jax
import jax.numpy as jnp
from jax import lax
from jax.experimental import pallas as pl
from jax.experimental.pallas import tpu as pltpu
from jax.sharding import PartitionSpec as P

BF16 = jnp.bfloat16
F32 = jnp.float32
MESH = pl.DeviceIdType.MESH
HEAD = 128
SCALE = HEAD ** (-0.5)
BLOCK = 64
NLEN = 128


class Pool:
    def __init__(self):
        self.used = 0

    def take(self, count):
        first = self.used
        self.used += count
        return first


POOL = Pool()
S_W = POOL.take(40)
S_KV = POOL.take(32)
S_DO = POOL.take(8)
S_ID = POOL.take(8)
S_HID = POOL.take(1)
S_Q = POOL.take(4)
S_HS = POOL.take(4)
S_HF = POOL.take(4)
S_ATT = POOL.take(16)
S_DQ = POOL.take(8)
S_DKV = POOL.take(32)
S_DH = POOL.take(1)
S_RS = POOL.take(16)
S_LOCAL = POOL.take(16)
N_SEMS = POOL.used


def dot(a, b, dims=((1,), (0,))):
    return lax.dot_general(a, b, (dims, ((), ())), preferred_element_type=F32)


def kernel(
    hidden, weight, keys, values, ids, grads,
    att_out, dh_out, dwq_out, dk_out, dv_out,
    hid, wb, kh0, kh1, vh0, vh1, doh, qh, qacc, qs, hs, ht, ck, cv, dks, dvs, atth, dqg, dqc, pw, rsb,
    dhs, dhr, dho, idg, ids_s, ssem, rsem,
):
    dp = lax.axis_index("dp")
    seq = lax.axis_index("seq")
    x, z = dp // 4, dp % 4
    y, c = seq // 2, seq % 2
    half = c * 1024
    kh, vh = (kh0, kh1), (vh0, vh1)

    def remote(src, dst, sem, to):
        return pltpu.make_async_remote_copy(
            src_ref=src, dst_ref=dst, send_sem=ssem.at[sem], recv_sem=rsem.at[sem],
            device_id=to, device_id_type=MESH,
        )

    def local(src, dst, sem):
        return pltpu.make_async_copy(src, dst, ssem.at[S_LOCAL + sem])

    def peer(dy, dc):
        return ((y + dy + 4) % 4) * 2 + (c + dc) % 2

    def cols(seq_of, h):
        return pl.multiple_of(((seq_of % 2) * 8 + (seq_of // 2) * 2 + h) * HEAD, HEAD)

    sibling = peer(0, 1)
    others = [(dy, dc) for dy in (1, 3, 2, 0) for dc in (0, 1) if (dy, dc) != (0, 0)]

    own_w = local(weight.at[:, pl.ds(pl.multiple_of(half, 1024), 1024)], wb.at[dp], 0)
    own_hid = local(hidden, hid.at[pl.ds(pl.multiple_of(c * 128, 128), 128)], 1)
    own_w.start()
    own_hid.start()
    rows4 = pl.ds(seq * 4, 4)
    own_kv = []
    for h in range(2):
        for i, (src, dst) in enumerate(((keys, kh), (values, vh))):
            own_kv.append(local(src.at[:, :, pl.ds(cols(seq, h), HEAD)], dst[h].at[rows4], 2 + 2 * h + i))
            own_kv[-1].start()
    own_tokens = pl.ds(pl.multiple_of(seq * 128, 128), 128)
    own_do = local(grads.at[:, pl.ds(cols(seq, 0), 2 * HEAD)], doh.at[own_tokens], 6)
    own_do.start()

    barrier = pltpu.get_barrier_semaphore()

    def greet(to):
        pl.semaphore_signal(barrier, inc=1, device_id=to, device_id_type=MESH)

    around = [
        (((x + 1) % 4) * 4 + z, seq), (((x + 3) % 4) * 4 + z, seq),
        (x * 4 + (z + 1) % 4, seq), (x * 4 + (z + 3) % 4, seq),
    ]
    for to in around:
        greet(to)
    for dy, dc in others:
        greet((dp, peer(dy, dc)))
    sender_core = dp // 8

    @pl.loop(0, 16)
    def _(k):
        @pl.when(jnp.logical_or(k != dp, c != sender_core))
        def _():
            greet((k, y * 2 + sender_core))

    own_block = jnp.where(c == sender_core, 1, 0)
    pl.semaphore_wait(barrier, 4 + 7 + 16 - own_block)

    def moved(axis, step):
        if axis == 0:
            return (((x + step + 4) % 4) * 4 + z, seq)
        return (x * 4 + (z + step + 4) % 4, seq)

    def source(t, r1, r2):
        rx, rz = (r1, r2) if t == 0 else (r2, r1)
        return ((x + rx + 4) % 4) * 4 + (z + rz + 4) % 4

    LINE = (0, -1, 1, 2)

    def piece(t, r1, r2, part):
        lo, n = {"all": (0, 128), "lo": (0, 64), "hi": (64, 64)}[part]
        return wb.at[source(t, r1, r2), pl.ds(t * 128 + lo, n)]

    def w_copy(t, phase, q, slot):
        axis = t if phase == 1 else 1 - t
        sem = S_W + 20 * t + (slot if phase == 1 else 4 + 4 * q + slot)
        step = 1 if slot % 2 == 0 else -1
        near = 0 if slot < 2 else -step
        part = "all" if slot < 2 else ("lo" if slot == 2 else "hi")
        src = piece(t, near, 0, part) if phase == 1 else piece(t, LINE[q], near, part)
        return remote(src, src, sem, moved(axis, step))

    def w_recv(t, phase, q, slot):
        axis = t if phase == 1 else 1 - t
        sem = S_W + 20 * t + (slot if phase == 1 else 4 + 4 * q + slot)
        step = 1 if slot % 2 == 0 else -1
        far = -step if slot < 2 else -2 * step
        part = "all" if slot < 2 else ("lo" if slot == 2 else "hi")
        if far == -2:
            far = 2
        dst = piece(t, far, 0, part) if phase == 1 else piece(t, LINE[q], far, part)
        remote(dst, dst, sem, moved(axis, step)).wait_recv()

    sent = []

    def go(copy):
        copy.start()
        sent.append(copy)

    own_w.wait()
    for t in (0, 1):
        for slot in (0, 1):
            go(w_copy(t, 1, 0, slot))
    for t in (0, 1):
        for slot in (0, 1):
            go(w_copy(t, 2, 0, slot))

    for j, (dy, dc) in enumerate(others):
        go(remote(ids, idg.at[seq], S_ID + j, (dp, peer(dy, dc))))
    own_hid.wait()
    own_hid_rows = hid.at[pl.ds(pl.multiple_of(c * 128, 128), 128)]
    hid_copy = remote(own_hid_rows, own_hid_rows, S_HID, (dp, sibling))
    go(hid_copy)

    def kv_sem(h, i, j):
        return S_KV + (h * 2 + i) * 8 + j

    for h in range(2):
        for i, (src, dst) in enumerate(((keys, kh), (values, vh))):
            for j, (dy, dc) in enumerate(others):
                to = peer(dy, dc)
                go(remote(src.at[:, :, pl.ds(cols(to, h), HEAD)], dst[h].at[rows4], kv_sem(h, i, j), (dp, to)))
        if h == 0:
            for j, (dy, dc) in enumerate(others):
                to = peer(dy, dc)
                go(remote(grads.at[:, pl.ds(cols(to, 0), 2 * HEAD)], doh.at[own_tokens], S_DO + j, (dp, to)))

    for t in (0, 1):
        for slot, q in ((0, 1), (1, 2)):
            w_recv(t, 1, 0, slot)
            go(w_copy(t, 1, 0, slot + 2))
            for s in (0, 1):
                go(w_copy(t, 2, q, s))
    for t in (0, 1):
        for slot in (0, 1):
            w_recv(t, 2, 0, slot)
            go(w_copy(t, 2, 0, slot + 2))
    other_rows = hid.at[pl.ds(pl.multiple_of((1 - c) * 128, 128), 128)]
    remote(other_rows, other_rows, S_HID, (dp, sibling)).wait_recv()
    for t in (0, 1):
        for slot in (2, 3):
            w_recv(t, 1, 0, slot)
        for s in (0, 1):
            go(w_copy(t, 2, 3, s))
    for q in (1, 2):
        for t in (0, 1):
            for slot in (0, 1):
                w_recv(t, 2, q, slot)
                go(w_copy(t, 2, q, slot + 2))

    def project(rx, first):
        @pl.loop(0, 4)
        def _(i):
            d = ((x + rx + 4) % 4) * 4 + i
            rows = hid[:, pl.ds(pl.multiple_of(d * 256, 256), 256)]
            for n in range(4):
                span = slice(n * 256, n * 256 + 256)
                part = dot(rows, wb[d, :, span])
                if first:
                    qacc[:, span] = jnp.where(i == 0, part, qacc[:, span] + part)
                else:
                    qacc[:, span] += part

    qacc[...] = jnp.zeros_like(qacc)
    for t in (0, 1):
        for slot in (0, 1):
            w_recv(t, 2, 3, slot)
            go(w_copy(t, 2, 3, slot + 2))
    for slot in (2, 3):
        w_recv(0, 2, 0, slot)
    project(0, False)
    for slot in (2, 3):
        w_recv(0, 2, 1, slot)
    project(-1, False)
    for slot in (2, 3):
        w_recv(0, 2, 2, slot)
    project(1, False)
    for slot in (2, 3):
        w_recv(0, 2, 3, slot)
        for q in range(4):
            w_recv(1, 2, q, slot)
    project(2, False)
    qs[...] = qacc[...].astype(BF16)

    def span256(k):
        return pl.ds(pl.multiple_of(k * 256, 256), 256)

    for dy in (1, 3, 2):
        to = peer(dy, 0)
        go(remote(qs.at[:, span256(to // 2)], qh.at[span256(y)], S_Q + dy, (dp, to)))
    qh[span256(y), :] = qs[:, span256(y)]

    def feats(k):
        return pl.ds(pl.multiple_of(k * 1024, 1024), 1024)

    def tokens(s):
        return pl.ds(pl.multiple_of(s * 128, 128), 128)

    for dy in (1, 3, 2):
        to = peer(dy, 0)
        go(remote(own_hid_rows.at[:, feats(to // 2)], hs.at[own_tokens], S_HS + dy, (dp, to)))
    hs[span256(y), :] = hid[:, feats(y)]

    for j, (dy, dc) in enumerate(others):
        frm = peer(-dy, -dc + 2)
        remote(ids, idg.at[frm], S_ID + j, (dp, frm)).wait_recv()
    idg[seq] = ids[...]
    to_smem = local(idg, ids_s, 7)
    to_smem.start()
    to_smem.wait()
    for j, (dy, dc) in enumerate(others):
        frm = peer(-dy, -dc + 2)
        dst = doh.at[tokens(frm)]
        remote(dst, dst, S_DO + j, (dp, frm)).wait_recv()
    own_do.wait()
    for cp in own_kv:
        cp.wait()

    def wait_kv(h):
        for i, dst in enumerate((kh, vh)):
            for j, (dy, dc) in enumerate(others):
                frm = peer(-dy, -dc + 2)
                ref = dst[h].at[pl.ds(frm * 4, 4)]
                remote(ref, ref, kv_sem(h, i, j), (dp, frm)).wait_recv()

    wait_kv(0)
    for dy in (1, 3, 2):
        frm = peer(-dy, 0)
        ref = qh.at[span256(frm // 2)]
        remote(ref, ref, S_Q + dy, (dp, frm)).wait_recv()

    ck[32] = jnp.zeros((NLEN, HEAD), BF16)
    cv[32] = jnp.zeros((NLEN, HEAD), BF16)

    def attend(h):
        lanes = slice(h * HEAD, h * HEAD + HEAD)

        @pl.loop(0, 8)
        def _(s):
            for u in range(2):
                rows = pl.ds(pl.multiple_of(s * 128 + u * BLOCK, BLOCK), BLOCK)
                first, second = ids_s[s, 0, 2 * u], ids_s[s, 0, 2 * u + 1]
                k = jnp.concatenate([kh[h][first], kh[h][second]], axis=0)
                v = jnp.concatenate([vh[h][first], vh[h][second]], axis=0)
                q = qh[rows, lanes]
                g = doh[rows, lanes]
                scores = dot(q, k, ((1,), (1,))) * SCALE
                peak = jnp.max(scores, axis=-1, keepdims=True)
                expo = jnp.exp(scores - peak)
                probs = expo / jnp.sum(expo, axis=-1, keepdims=True)
                low = probs.astype(BF16)
                atth[h, rows] = dot(low, v).astype(BF16)
                d_probs = dot(g, v, ((1,), (1,)))
                delta = jnp.sum(probs * d_probs, axis=-1, keepdims=True)
                d_scores = (probs * (d_probs - delta) * SCALE).astype(BF16)
                dqg[h, y, rows] = dot(d_scores, k).astype(BF16)
                dk = dot(d_scores, q, ((0,), (0,))).astype(BF16)
                dv = dot(low, g, ((0,), (0,))).astype(BF16)
                for i in range(2):
                    ck[s * 4 + 2 * u + i] = dk[i * NLEN:(i + 1) * NLEN]
                    cv[s * 4 + 2 * u + i] = dv[i * NLEN:(i + 1) * NLEN]

    def dq_copy(h, slot):
        step = 1 if slot % 2 == 0 else -1
        near = y if slot < 2 else (y - step + 4) % 4
        rows = {0: pl.ds(0, 1024), 1: pl.ds(0, 1024), 2: pl.ds(0, 512), 3: pl.ds(512, 512)}[slot]
        ref = dqg.at[h, near, rows]
        return remote(ref, ref, S_DQ + 4 * h + slot, (dp, peer(step, 0)))

    def dq_recv(h, slot):
        step = 1 if slot % 2 == 0 else -1
        far = (y - step + 4) % 4 if slot < 2 else (y + 2) % 4
        rows = {0: pl.ds(0, 1024), 1: pl.ds(0, 1024), 2: pl.ds(0, 512), 3: pl.ds(512, 512)}[slot]
        ref = dqg.at[h, far, rows]
        remote(ref, ref, S_DQ + 4 * h + slot, (dp, peer(step, 0))).wait_recv()

    def dkv_copy(h, i, j):
        dy, dc = j // 2, j % 2
        to = peer(dy, dc)
        src, dst = ((dks, dk_out), (dvs, dv_out))[i]
        return remote(
            src.at[h, pl.ds(to * 4, 4)], dst.at[:, :, pl.ds(cols(seq, h), HEAD)],
            S_DKV + (h * 2 + i) * 8 + j, (dp, to),
        )

    def return_kv(h):
        def accumulate(to):
            @pl.loop(0, 4)
            def _(r):
                row = to * 4 + r
                total_k = jnp.zeros((NLEN, HEAD), F32)
                total_v = jnp.zeros((NLEN, HEAD), F32)
                for s in range(8):
                    at = jnp.int32(32)
                    for j in range(4):
                        at = jnp.where(ids_s[s, 0, j] == row, 4 * s + j, at)
                    total_k += ck[at].astype(F32)
                    total_v += cv[at].astype(F32)
                dks[h, row] = total_k.astype(BF16)
                dvs[h, row] = total_v.astype(BF16)

        @pl.loop(0, 8)
        def _(jj):
            j = (jj + 1) % 8
            accumulate(peer(j // 2, j % 2))

            @pl.when(j != 0)
            def _():
                for i in range(2):
                    dkv_copy(h, i, j).start()

        for i, (src, dst) in enumerate(((dks, dk_out), (dvs, dv_out))):
            local(src.at[h, rows4], dst.at[:, :, pl.ds(cols(seq, h), HEAD)], 8 + 2 * h + i).start()

    def att_copy(h, j):
        dy, dc = others[j]
        to = peer(dy, dc)
        return remote(
            atth.at[h, tokens(to)], att_out.at[:, pl.ds(cols(seq, h), HEAD)],
            S_ATT + 8 * h + j, (dp, to),
        )

    def forward_hidden():
        for dy in (1, 3, 2):
            frm = peer(-dy, 0)
            ref = hs.at[tokens(frm)]
            remote(ref, ref, S_HS + dy, (dp, frm)).wait_recv()
            go(remote(ref, ref, S_HF + dy, (dp, sibling)))

    attend(0)
    for slot in (0, 1):
        go(dq_copy(0, slot))
    forward_hidden()
    return_kv(0)
    wait_kv(1)
    attend(1)
    for slot in (0, 1):
        go(dq_copy(1, slot))
    for slot in (0, 1):
        dq_recv(0, slot)
        go(dq_copy(0, slot + 2))
    return_kv(1)
    for slot in (0, 1):
        dq_recv(1, slot)
        go(dq_copy(1, slot + 2))
    for h in range(2):
        for j in range(7):
            go(att_copy(h, j))
        local(atth.at[h, own_tokens], att_out.at[:, pl.ds(cols(seq, h), HEAD)], 12 + h).start()

    for dy in (1, 3, 2):
        frm = peer(-dy, 1)
        ref = hs.at[tokens(frm)]
        remote(ref, ref, S_HF + dy, (dp, sibling)).wait_recv()

    @pl.loop(0, 4)
    def _(m):
        ht[span256(m), :] = jnp.transpose(hs[:, span256(m)])

    def rs_copy(i, other_core):
        to_core = (c + other_core) % 2
        return remote(
            pw.at[i, pl.ds(pl.multiple_of(to_core * 512, 512), 512)], rsb.at[dp],
            S_RS + 0, (8 * c + i, y * 2 + to_core),
        )

    def rs_send(i, other_core):
        to_core = (c + other_core) % 2
        return pltpu.make_async_remote_copy(
            src_ref=pw.at[i, pl.ds(pl.multiple_of(to_core * 512, 512), 512)], dst_ref=rsb.at[dp],
            send_sem=ssem.at[S_RS + 2 * i + other_core], recv_sem=rsem.at[S_RS + dp],
            device_id=(8 * c + i, y * 2 + to_core), device_id_type=MESH,
        )

    def own_rs():
        return local(
            pw.at[dp % 8, pl.ds(pl.multiple_of(c * 512, 512), 512)], rsb.at[dp], 14
        )

    def weight_grad(dy):
        yy = (y + dy) % 4
        both = jnp.concatenate([dqg[0, yy], dqg[1, yy]], axis=1)
        for m in range(4):
            out = dot(ht[m * 256:m * 256 + 256, :], both).astype(BF16)
            for h in range(2):
                pw[2 * yy + h, m * 256:m * 256 + 256] = out[:, h * HEAD:(h + 1) * HEAD]
        for h in range(2):
            i = 2 * yy + h
            for other_core in range(2):
                mine = jnp.logical_and(8 * c + i == dp, other_core == 0)

                @pl.when(jnp.logical_not(mine))
                def _():
                    rs_send(i, other_core).start()

    weight_grad(0)
    weight_grad(3)
    weight_grad(1)
    for h in range(2):
        for slot in (2, 3):
            dq_recv(h, slot)
    weight_grad(2)

    @pl.when(own_block == 1)
    def _():
        own_rs().start()

    for yy in range(4):
        for h in range(2):
            dqc[:, (2 * yy + h) * HEAD:(2 * yy + h + 1) * HEAD] = dqg[h, yy, span256(y)]

    @pl.loop(0, 16)
    def _(d):
        theirs = dot(dqc[pl.ds(pl.multiple_of((1 - c) * 128, 128), 128), :], wb[d], ((1,), (1,)))
        dhs[:, span256(d)] = theirs
        ours = dot(dqc[pl.ds(pl.multiple_of(c * 128, 128), 128), :], wb[d], ((1,), (1,)))
        dho[:, span256(d)] = ours

    dh_copy = remote(dhs, dhr, S_DH, (dp, sibling))
    dh_copy.start()
    sent.append(dh_copy)
    dh_copy.wait_recv()
    dh_out[...] = (dho[...] + dhr[...]).astype(BF16)

    @pl.when(own_block == 1)
    def _():
        own_rs().wait()

    @pl.loop(0, 16)
    def _(k):
        @pl.when(jnp.logical_or(k != dp, own_block == 0))
        def _():
            pltpu.make_async_remote_copy(
                src_ref=rsb.at[k], dst_ref=rsb.at[k], send_sem=ssem.at[S_RS], recv_sem=rsem.at[S_RS + k],
                device_id=(dp, sibling), device_id_type=MESH,
            ).wait_recv()

    total = rsb[0].astype(F32)
    for k in range(1, 16):
        total += rsb[k].astype(F32)
    dwq_out[...] = total

    for h in range(2):
        for j in range(7):
            att_copy(h, j).wait_recv()
        local(atth.at[h, own_tokens], att_out.at[:, pl.ds(cols(seq, h), HEAD)], 12 + h).wait()
        for i, (src, dst) in enumerate(((dks, dk_out), (dvs, dv_out))):
            local(src.at[h, rows4], dst.at[:, :, pl.ds(cols(seq, h), HEAD)], 8 + 2 * h + i).wait()

            @pl.loop(1, 8)
            def _(j):
                frm = peer(4 - j // 2, 2 - j % 2)
                ref = dst.at[:, :, pl.ds(cols(frm, h), HEAD)]
                remote(src.at[h, pl.ds(frm * 4, 4)], ref, S_DKV + (h * 2 + i) * 8 + j, (dp, frm)).wait_recv()
                dkv_copy(h, i, j).wait_send()

    @pl.loop(0, 8)
    def _(i):
        for other_core in range(2):
            mine = jnp.logical_and(8 * c + i == dp, other_core == 0)

            @pl.when(jnp.logical_not(mine))
            def _():
                rs_send(i, other_core).wait_send()

    for copy in sent:
        copy.wait_send()


def on_device(hidden, w_query, nbr_keys, nbr_values, nbr_ids, d_attended):
    ids = jnp.pad(nbr_ids.reshape(1, 4), ((0, 7), (0, 124)))
    vmem = pltpu.VMEM
    anywhere = pl.BlockSpec(memory_space=pl.ANY)
    in_vmem = pl.BlockSpec(memory_space=pltpu.VMEM)
    attended, d_hidden, d_wq, d_keys, d_values = pl.pallas_call(
        kernel,
        out_shape=(
            jax.ShapeDtypeStruct((128, 2048), BF16),
            jax.ShapeDtypeStruct((128, 4096), BF16),
            jax.ShapeDtypeStruct((512, 128), F32),
            jax.ShapeDtypeStruct((4, 128, 2048), BF16),
            jax.ShapeDtypeStruct((4, 128, 2048), BF16),
        ),
        in_specs=[anywhere, anywhere, anywhere, anywhere, in_vmem, anywhere],
        out_specs=(anywhere, in_vmem, in_vmem, anywhere, anywhere),
        scratch_shapes=[
            vmem((256, 4096), BF16),
            vmem((16, 256, 1024), BF16),
            *[vmem((32, 128, 128), BF16)] * 4,
            vmem((1024, 256), BF16),
            vmem((1024, 256), BF16),
            vmem((256, 1024), F32),
            vmem((256, 1024), BF16),
            vmem((1024, 1024), BF16),
            vmem((1024, 1024), BF16),
            vmem((33, 128, 128), BF16),
            vmem((33, 128, 128), BF16),
            vmem((2, 32, 128, 128), BF16),
            vmem((2, 32, 128, 128), BF16),
            vmem((2, 1024, 128), BF16),
            vmem((2, 4, 1024, 128), BF16),
            vmem((256, 1024), BF16),
            vmem((8, 1024, 128), BF16),
            vmem((16, 512, 128), BF16),
            vmem((128, 4096), F32),
            vmem((128, 4096), F32),
            vmem((128, 4096), F32),
            vmem((8, 8, 128), jnp.int32),
            pltpu.SMEM((8, 8, 128), jnp.int32),
            pltpu.SemaphoreType.DMA((N_SEMS,)),
            pltpu.SemaphoreType.DMA((N_SEMS,)),
        ],
        compiler_params=pltpu.CompilerParams(
            collective_id=0, has_side_effects=True, vmem_limit_bytes=60 * 2**20
        ),
        name="group_attention",
    )(hidden, w_query, nbr_keys, nbr_values, ids, d_attended)
    return attended, d_hidden, d_wq, d_keys.astype(F32), d_values.astype(F32)


def solution(mesh):
    placed = (
        P(("dp", "seq"), None),
        P("dp", None),
        P(("dp", "seq"), None, None),
        P(("dp", "seq"), None, None),
        P(("dp", "seq"), None),
        P(("dp", "seq"), None),
    )
    return jax.shard_map(
        on_device,
        mesh=mesh,
        in_specs=placed,
        out_specs=(
            P(("dp", "seq"), None),
            P(("dp", "seq"), None),
            P("seq", "dp"),
            P(("dp", "seq"), None, None),
            P(("dp", "seq"), None, None),
        ),
        check_vma=False,
    )
```

time: 388 us -> 184 us (0.47)
  the two profiles are of different devices: /device:TPU:1 before, /device:TPU:35 now
where the time goes in v1:
time: 184 us
  Pallas kernels  172 us (93%)
  other arithmetic  6.82 us (4%)
  local copies, waits for them, and re-layouts  3.84 us (2%)
    pallas_call x1, Pallas kernels, on_device(): pl.pallas_call(kernel, out_shape=(jax.ShapeDtypeStruct((128, 2048), BF16)...  172 us
    convert_element_type x2, other arithmetic, on_device(): return (attended, d_hidden, d_wq, d_keys.astype(F32), d_values.astype(F32))  6.82 us

profile of v1, /device:TPU:35, one launch (start us, length us, event | category | flops | bytes accessed | tf_op | source)
XLA Modules:
  0.0 183.6 jit_solution(13442224068640988126)
XLA Ops:
  0.6 0.8 reshape.13
  1.4 0.6 pad.4.ids
  2.0 172.3 %group_attention.1 = (bf16[128,2048]{1,0:T(8,128)(2,1)}, bf16[128,4096]{1,0:T(8,128)(2,1)}, f32[512,128]{1,0:T(8,128)}, bf16[4,128,2048]{2,1,0:T(8,128)(2,1)}, bf16[4,128,2048]{2,1,0:T(8,128)(2,1)}) custom-call(bf16[128,4096]{1,0:T(8,128)(2,1)} %hidden.1, bf16[256,2048]{1,0:T(8,128)(2,1)} %weight.1, bf16[4,128,2048]{2,1,0:T(8,128)(2,1)} %keys.1, ...), custom_call_target="tpu_custom_call" | custom-call | tf_op jit(solution)/shard_map/group_attention/pallas_call | solution.py:536
  174.3 0.0 copy-start
  174.3 4.3 %convert_element_type.6 = f32[4,128,2048]{2,1,0:T(8,128)} convert(bf16[4,128,2048]{2,1,0:T(8,128)(2,1)} %get-tuple-element.13) | non-fusion elementwise | flops 1048576 | bytes 6291456 | tf_op jit(solution)/shard_map/convert_element_type | solution.py:579
  178.6 0.0 copy-done
  178.6 0.0 copy-start.2
  178.6 0.0 copy-start.1
  178.6 2.5 %convert_element_type.7 = f32[4,128,2048]{2,1,0:T(8,128)} convert(bf16[4,128,2048]{2,1,0:T(8,128)(2,1)S(1)} %copy-done) | non-fusion elementwise | flops 1048576 | bytes 6291456 | tf_op jit(solution)/shard_map/convert_element_type | solution.py:579
  181.1 0.0 copy-done.2
  181.1 0.0 copy-start.3
  181.1 0.8 copy.14
  181.9 0.0 copy-done.1
  181.9 1.0 copy.15
  182.9 0.0 copy-done.3
  182.9 0.7 copy.16
Async XLA Ops:
  174.3 4.3 %copy-start = (bf16[4,128,2048]{2,1,0:T(8,128)(2,1)S(1)}, bf16[4,128,2048]{2,1,0:T(8,128)(2,1)}, u32[]{:S(2)}) copy-start(bf16[4,128,2048]{2,1,0:T(8,128)(2,1)} %get-tuple-element.14) | copy-start | bytes 6291460
  178.6 2.5 %copy-start.2 = (bf16[128,2048]{1,0:T(8,128)(2,1)S(1)}, bf16[128,2048]{1,0:T(8,128)(2,1)}, u32[]{:S(2)}) copy-start(bf16[128,2048]{1,0:T(8,128)(2,1)} %get-tuple-element.20) | copy-start | bytes 1572868
  178.6 3.3 %copy-start.1 = (bf16[128,4096]{1,0:T(8,128)(2,1)S(1)}, bf16[128,4096]{1,0:T(8,128)(2,1)}, u32[]{:S(2)}) copy-start(bf16[128,4096]{1,0:T(8,128)(2,1)} %get-tuple-element.21) | copy-start | bytes 3145732
  181.1 1.8 copy-start.3

commit v2 on v1

--- a/solution.py
+++ b/solution.py
@@ -39,7 +39,8 @@
 S_DQ = POOL.take(8)
 S_DKV = POOL.take(32)
 S_DH = POOL.take(1)
-S_RS = POOL.take(16)
+S_R1 = POOL.take(8)
+S_R2 = POOL.take(4)
 S_LOCAL = POOL.take(16)
 N_SEMS = POOL.used
 
@@ -51,7 +52,7 @@
 def kernel(
     hidden, weight, keys, values, ids, grads,
     att_out, dh_out, dwq_out, dk_out, dv_out,
-    hid, wb, kh0, kh1, vh0, vh1, doh, qh, qacc, qs, hs, ht, ck, cv, dks, dvs, atth, dqg, dqc, pw, rsb,
+    hid, wb, kh0, kh1, vh0, vh1, doh, qh, qacc, qs, hs, ht, ck, cv, dks, dvs, atth, dqg, dqc, pw, r1, r1s, r2,
     dhs, dhr, dho, idg, ids_s, ssem, rsem,
 ):
     dp = lax.axis_index("dp")
@@ -98,24 +99,13 @@
     def greet(to):
         pl.semaphore_signal(barrier, inc=1, device_id=to, device_id_type=MESH)
 
-    around = [
-        (((x + 1) % 4) * 4 + z, seq), (((x + 3) % 4) * 4 + z, seq),
-        (x * 4 + (z + 1) % 4, seq), (x * 4 + (z + 3) % 4, seq),
-    ]
-    for to in around:
-        greet(to)
     for dy, dc in others:
         greet((dp, peer(dy, dc)))
-    sender_core = dp // 8
-
-    @pl.loop(0, 16)
-    def _(k):
-        @pl.when(jnp.logical_or(k != dp, c != sender_core))
-        def _():
-            greet((k, y * 2 + sender_core))
-
-    own_block = jnp.where(c == sender_core, 1, 0)
-    pl.semaphore_wait(barrier, 4 + 7 + 16 - own_block)
+    for step in (1, 2, 3):
+        for core in (0, 1):
+            greet((((x + step) % 4) * 4 + z, y * 2 + core))
+            greet((x * 4 + (z + step) % 4, y * 2 + core))
+    pl.semaphore_wait(barrier, 7 + 12)
 
     def moved(axis, step):
         if axis == 0:
@@ -176,15 +166,13 @@
     def kv_sem(h, i, j):
         return S_KV + (h * 2 + i) * 8 + j
 
-    for h in range(2):
-        for i, (src, dst) in enumerate(((keys, kh), (values, vh))):
-            for j, (dy, dc) in enumerate(others):
-                to = peer(dy, dc)
-                go(remote(src.at[:, :, pl.ds(cols(to, h), HEAD)], dst[h].at[rows4], kv_sem(h, i, j), (dp, to)))
-        if h == 0:
-            for j, (dy, dc) in enumerate(others):
-                to = peer(dy, dc)
-                go(remote(grads.at[:, pl.ds(cols(to, 0), 2 * HEAD)], doh.at[own_tokens], S_DO + j, (dp, to)))
+    def send_kv(h, i):
+        src, dst = ((keys, kh), (values, vh))[i]
+        for j, (dy, dc) in enumerate(others):
+            to = peer(dy, dc)
+            go(remote(src.at[:, :, pl.ds(cols(to, h), HEAD)], dst[h].at[rows4], kv_sem(h, i, j), (dp, to)))
+
+    send_kv(0, 0)
 
     for t in (0, 1):
         for slot, q in ((0, 1), (1, 2)):
@@ -192,10 +180,14 @@
             go(w_copy(t, 1, 0, slot + 2))
             for s in (0, 1):
                 go(w_copy(t, 2, q, s))
+    send_kv(0, 1)
     for t in (0, 1):
         for slot in (0, 1):
             w_recv(t, 2, 0, slot)
             go(w_copy(t, 2, 0, slot + 2))
+    for j, (dy, dc) in enumerate(others):
+        to = peer(dy, dc)
+        go(remote(grads.at[:, pl.ds(cols(to, 0), 2 * HEAD)], doh.at[own_tokens], S_DO + j, (dp, to)))
     other_rows = hid.at[pl.ds(pl.multiple_of((1 - c) * 128, 128), 128)]
     remote(other_rows, other_rows, S_HID, (dp, sibling)).wait_recv()
     for t in (0, 1):
@@ -203,6 +195,7 @@
             w_recv(t, 1, 0, slot)
         for s in (0, 1):
             go(w_copy(t, 2, 3, s))
+    send_kv(1, 0)
     for q in (1, 2):
         for t in (0, 1):
             for slot in (0, 1):
@@ -227,6 +220,7 @@
         for slot in (0, 1):
             w_recv(t, 2, 3, slot)
             go(w_copy(t, 2, 3, slot + 2))
+    send_kv(1, 1)
     for slot in (2, 3):
         w_recv(0, 2, 0, slot)
     project(0, False)
@@ -344,7 +338,7 @@
             S_DKV + (h * 2 + i) * 8 + j, (dp, to),
         )
 
-    def return_kv(h):
+    def sum_kv(h):
         def accumulate(to):
             @pl.loop(0, 4)
             def _(r):
@@ -361,17 +355,16 @@
                 dvs[h, row] = total_v.astype(BF16)
 
         @pl.loop(0, 8)
-        def _(jj):
-            j = (jj + 1) % 8
-            accumulate(peer(j // 2, j % 2))
-
-            @pl.when(j != 0)
-            def _():
-                for i in range(2):
-                    dkv_copy(h, i, j).start()
-
-        for i, (src, dst) in enumerate(((dks, dk_out), (dvs, dv_out))):
-            local(src.at[h, rows4], dst.at[:, :, pl.ds(cols(seq, h), HEAD)], 8 + 2 * h + i).start()
+        def _(to):
+            accumulate(to)
+
+    def send_dkv(h, i):
+        @pl.loop(1, 8)
+        def _(j):
+            dkv_copy(h, i, j).start()
+
+        src, dst = ((dks, dk_out), (dvs, dv_out))[i]
+        local(src.at[h, rows4], dst.at[:, :, pl.ds(cols(seq, h), HEAD)], 8 + 2 * h + i).start()
 
     def att_copy(h, j):
         dy, dc = others[j]
@@ -391,8 +384,9 @@
     attend(0)
     for slot in (0, 1):
         go(dq_copy(0, slot))
+    sum_kv(0)
+    send_dkv(0, 0)
     forward_hidden()
-    return_kv(0)
     wait_kv(1)
     attend(1)
     for slot in (0, 1):
@@ -400,71 +394,82 @@
     for slot in (0, 1):
         dq_recv(0, slot)
         go(dq_copy(0, slot + 2))
-    return_kv(1)
+    send_dkv(0, 1)
+    sum_kv(1)
     for slot in (0, 1):
         dq_recv(1, slot)
         go(dq_copy(1, slot + 2))
+    send_dkv(1, 0)
+
+    for dy in (1, 3, 2):
+        frm = peer(-dy, 1)
+        ref = hs.at[tokens(frm)]
+        remote(ref, ref, S_HF + dy, (dp, sibling)).wait_recv()
+
+    @pl.loop(0, 4)
+    def _(m):
+        ht[span256(m), :] = jnp.transpose(hs[:, span256(m)])
+
+    def wq_grad(k):
+        both = jnp.concatenate([dqg[0, k], dqg[1, k]], axis=1)
+        for m in range(4):
+            out = dot(ht[m * 256:m * 256 + 256, :], both).astype(BF16)
+            for h in range(2):
+                pw[k // 2, 2 * (k % 2) + h, m * 256:m * 256 + 256] = out[:, h * HEAD:(h + 1) * HEAD]
+
+    def r1_copy(core, to, part):
+        if core == 0:
+            src, slot, dest = pw.at[to, pl.ds(2 * part, 2), pl.ds(0, 512)], x, (2 * c + to) * 4 + z
+        else:
+            src, slot, dest = pw.at[:, to, pl.ds(512, 512)], z, x * 4 + to
+            part = c
+        dst = r1.at[slot, pl.ds(2 * part, 2)]
+        sem = ssem.at[S_R1 + (2 * to + part if core == 0 else 4 + to)]
+        own = jnp.logical_and(dest == dp, c == core)
+        return src, dst, sem, rsem.at[S_R1 + slot * 2 + part], (dest, y * 2 + core), own
+
+    def r1_start(core, to, part):
+        src, dst, s_sem, r_sem, dest, own = r1_copy(core, to, part)
+
+        @pl.when(own)
+        def _():
+            pltpu.make_async_copy(src, dst, s_sem).start()
+
+        @pl.when(jnp.logical_not(own))
+        def _():
+            pltpu.make_async_remote_copy(
+                src_ref=src, dst_ref=dst, send_sem=s_sem, recv_sem=r_sem, device_id=dest, device_id_type=MESH
+            ).start()
+
+    def r1_wait(core, to, part):
+        src, dst, s_sem, r_sem, dest, own = r1_copy(core, to, part)
+
+        @pl.when(own)
+        def _():
+            pltpu.make_async_copy(src, dst, s_sem).wait()
+
+        @pl.when(jnp.logical_not(own))
+        def _():
+            pltpu.make_async_remote_copy(
+                src_ref=src, dst_ref=dst, send_sem=s_sem, recv_sem=r_sem, device_id=dest, device_id_type=MESH
+            ).wait_send()
+
+    R1_ALL = [(0, to, part) for to in range(2) for part in range(2)] + [(1, to, 0) for to in range(4)]
+
+    for h in range(2):
+        for slot in (2, 3):
+            dq_recv(h, slot)
+    for k in range(4):
+        wq_grad(k)
+        r1_start(0, k // 2, k % 2)
+        if k >= 2:
+            r1_start(1, 2 * (k - 2), 0)
+            r1_start(1, 2 * (k - 2) + 1, 0)
+    send_dkv(1, 1)
     for h in range(2):
         for j in range(7):
             go(att_copy(h, j))
         local(atth.at[h, own_tokens], att_out.at[:, pl.ds(cols(seq, h), HEAD)], 12 + h).start()
-
-    for dy in (1, 3, 2):
-        frm = peer(-dy, 1)
-        ref = hs.at[tokens(frm)]
-        remote(ref, ref, S_HF + dy, (dp, sibling)).wait_recv()
-
-    @pl.loop(0, 4)
-    def _(m):
-        ht[span256(m), :] = jnp.transpose(hs[:, span256(m)])
-
-    def rs_copy(i, other_core):
-        to_core = (c + other_core) % 2
-        return remote(
-            pw.at[i, pl.ds(pl.multiple_of(to_core * 512, 512), 512)], rsb.at[dp],
-            S_RS + 0, (8 * c + i, y * 2 + to_core),
-        )
-
-    def rs_send(i, other_core):
-        to_core = (c + other_core) % 2
-        return pltpu.make_async_remote_copy(
-            src_ref=pw.at[i, pl.ds(pl.multiple_of(to_core * 512, 512), 512)], dst_ref=rsb.at[dp],
-            send_sem=ssem.at[S_RS + 2 * i + other_core], recv_sem=rsem.at[S_RS + dp],
-            device_id=(8 * c + i, y * 2 + to_core), device_id_type=MESH,
-        )
-
-    def own_rs():
-        return local(
-            pw.at[dp % 8, pl.ds(pl.multiple_of(c * 512, 512), 512)], rsb.at[dp], 14
-        )
-
-    def weight_grad(dy):
-        yy = (y + dy) % 4
-        both = jnp.concatenate([dqg[0, yy], dqg[1, yy]], axis=1)
-        for m in range(4):
-            out = dot(ht[m * 256:m * 256 + 256, :], both).astype(BF16)
-            for h in range(2):
-                pw[2 * yy + h, m * 256:m * 256 + 256] = out[:, h * HEAD:(h + 1) * HEAD]
-        for h in range(2):
-            i = 2 * yy + h
-            for other_core in range(2):
-                mine = jnp.logical_and(8 * c + i == dp, other_core == 0)
-
-                @pl.when(jnp.logical_not(mine))
-                def _():
-                    rs_send(i, other_core).start()
-
-    weight_grad(0)
-    weight_grad(3)
-    weight_grad(1)
-    for h in range(2):
-        for slot in (2, 3):
-            dq_recv(h, slot)
-    weight_grad(2)
-
-    @pl.when(own_block == 1)
-    def _():
-        own_rs().start()
 
     for yy in range(4):
         for h in range(2):
@@ -480,26 +485,42 @@
     dh_copy = remote(dhs, dhr, S_DH, (dp, sibling))
     dh_copy.start()
     sent.append(dh_copy)
+    for core, to, part in R1_ALL:
+        r1_wait(core, to, part)
+    line1, line2 = jnp.where(c == 0, x, z), jnp.where(c == 0, z, x)
+
+    @pl.loop(0, 8)
+    def _(k):
+        from_core = jnp.where(c == 0, x // 2, k % 2)
+
+        @pl.when(jnp.logical_not(jnp.logical_and(k // 2 == line1, from_core == c)))
+        def _():
+            ref = r1.at[k // 2, pl.ds(2 * (k % 2), 2)]
+            pltpu.make_async_remote_copy(
+                src_ref=ref, dst_ref=ref, send_sem=ssem.at[S_R1], recv_sem=rsem.at[S_R1 + k],
+                device_id=(dp, sibling), device_id_type=MESH,
+            ).wait_recv()
+
+    def r2_copy(step):
+        to = (line2 + step) % 4
+        dest = jnp.where(c == 0, line1 * 4 + to, to * 4 + line1)
+        return remote(r1s.at[to], r2.at[step], S_R2 + step, (dest, seq))
+
+    for step in (1, 3, 2, 0):
+        to = (line2 + step) % 4
+        total = r1[0, to].astype(F32)
+        for k in range(1, 4):
+            total += r1[k, to].astype(F32)
+        if step:
+            r1s[to] = total.astype(BF16)
+            go(r2_copy(step))
+        else:
+            dwq_out[...] = total
     dh_copy.wait_recv()
     dh_out[...] = (dho[...] + dhr[...]).astype(BF16)
-
-    @pl.when(own_block == 1)
-    def _():
-        own_rs().wait()
-
-    @pl.loop(0, 16)
-    def _(k):
-        @pl.when(jnp.logical_or(k != dp, own_block == 0))
-        def _():
-            pltpu.make_async_remote_copy(
-                src_ref=rsb.at[k], dst_ref=rsb.at[k], send_sem=ssem.at[S_RS], recv_sem=rsem.at[S_RS + k],
-                device_id=(dp, sibling), device_id_type=MESH,
-            ).wait_recv()
-
-    total = rsb[0].astype(F32)
-    for k in range(1, 16):
-        total += rsb[k].astype(F32)
-    dwq_out[...] = total
+    for step in (1, 3, 2):
+        r2_copy(step).wait_recv()
+        dwq_out[...] += r2[step].astype(F32)
 
     for h in range(2):
         for j in range(7):
@@ -515,17 +536,16 @@
                 remote(src.at[h, pl.ds(frm * 4, 4)], ref, S_DKV + (h * 2 + i) * 8 + j, (dp, frm)).wait_recv()
                 dkv_copy(h, i, j).wait_send()
 
-    @pl.loop(0, 8)
-    def _(i):
-        for other_core in range(2):
-            mine = jnp.logical_and(8 * c + i == dp, other_core == 0)
-
-            @pl.when(jnp.logical_not(mine))
-            def _():
-                rs_send(i, other_core).wait_send()
-
     for copy in sent:
         copy.wait_send()
+
+
+def finish(att_in, dh_in, dwq_in, dk_in, dv_in, att_out, dh_out, dwq_out, dk_out, dv_out):
+    att_out[...] = att_in[...]
+    dh_out[...] = dh_in[...]
+    dwq_out[...] = dwq_in[...]
+    dk_out[...] = dk_in[...].astype(F32)
+    dv_out[...] = dv_in[...].astype(F32)
 
 
 def on_device(hidden, w_query, nbr_keys, nbr_values, nbr_ids, d_attended):
@@ -561,8 +581,10 @@
             vmem((2, 1024, 128), BF16),
             vmem((2, 4, 1024, 128), BF16),
             vmem((256, 1024), BF16),
-            vmem((8, 1024, 128), BF16),
-            vmem((16, 512, 128), BF16),
+            vmem((2, 4, 1024, 128), BF16),
+            vmem((4, 4, 512, 128), BF16),
+            vmem((4, 512, 128), BF16),
+            vmem((4, 512, 128), BF16),
             vmem((128, 4096), F32),
             vmem((128, 4096), F32),
             vmem((128, 4096), F32),
@@ -576,7 +598,20 @@
         ),
         name="group_attention",
     )(hidden, w_query, nbr_keys, nbr_values, ids, d_attended)
-    return attended, d_hidden, d_wq, d_keys.astype(F32), d_values.astype(F32)
+    parts = (attended, d_hidden, d_wq, d_keys.reshape(512, 2048), d_values.reshape(512, 2048))
+    steps = 8
+    specs = [pl.BlockSpec((p.shape[0] // steps, p.shape[1]), lambda i: (i, 0)) for p in parts]
+    kinds = (BF16, BF16, F32, F32, F32)
+    attended, d_hidden, d_wq, d_keys, d_values = pl.pallas_call(
+        finish,
+        grid=(steps,),
+        out_shape=[jax.ShapeDtypeStruct(p.shape, kind) for p, kind in zip(parts, kinds)],
+        in_specs=specs,
+        out_specs=specs,
+        compiler_params=pltpu.CompilerParams(vmem_limit_bytes=60 * 2**20),
+        name="finish",
+    )(*parts)
+    return attended, d_hidden, d_wq, d_keys.reshape(4, 128, 2048), d_values.reshape(4, 128, 2048)
 
 
 def solution(mesh):

time: 184 us -> 163 us (0.89)
  the two profiles are of different devices: /device:TPU:35 before, /device:TPU:1 now
where the time goes in v2:
time: 163 us; the launch traced here: 161 us
  Pallas kernels  159 us (98%)
    pallas_call x1, Pallas kernels, on_device(): pl.pallas_call(kernel, out_shape=(jax.ShapeDtypeStruct((128, 2048), BF16)...  151 us
    pallas_call x1, Pallas kernels, on_device(): pl.pallas_call(finish, grid=(steps,), out_shape=[jax.ShapeDtypeStruct(p.s...  8.3 us

profile of v2, /device:TPU:1, one launch (start us, length us, event | category | flops | bytes accessed | tf_op | source)
XLA Modules:
  0.0 160.8 jit_solution(11077899137291082963)
XLA Ops:
  0.6 0.8 reshape.25
  1.4 0.6 pad.4.ids
  2.0 150.5 %group_attention.1 = (bf16[128,2048]{1,0:T(8,128)(2,1)}, bf16[128,4096]{1,0:T(8,128)(2,1)}, f32[512,128]{1,0:T(8,128)}, bf16[4,128,2048]{2,1,0:T(8,128)(2,1)}, bf16[4,128,2048]{2,1,0:T(8,128)(2,1)}) custom-call(bf16[128,4096]{1,0:T(8,128)(2,1)} %hidden.1, bf16[256,2048]{1,0:T(8,128)(2,1)} %weight.1, bf16[4,128,2048]{2,1,0:T(8,128)(2,1)} %keys.1, ...), custom_call_target="tpu_custom_call" | custom-call | tf_op jit(solution)/shard_map/group_attention/pallas_call | solution.py:556
  152.5 8.3 %finish.1 = (bf16[128,2048]{1,0:T(8,128)(2,1)}, bf16[128,4096]{1,0:T(8,128)(2,1)}, f32[512,128]{1,0:T(8,128)}, f32[512,2048]{1,0:T(8,128)}, f32[512,2048]{1,0:T(8,128)}) custom-call(bf16[128,2048]{1,0:T(8,128)(2,1)} %get-tuple-element.15.att_in, bf16[128,4096]{1,0:T(8,128)(2,1)} %get-tuple-element.16.dh_in, f32[512,128]{1,0:T(8,128)} %get-tuple-element.17.dwq_in, ...), custom_call_target="tpu_custom_call" | custom-call | tf_op jit(solution)/shard_map/finish/pallas_call | solution.py:605

commit v3 on v2

--- a/solution.py
+++ b/solution.py
@@ -53,7 +53,7 @@
     hidden, weight, keys, values, ids, grads,
     att_out, dh_out, dwq_out, dk_out, dv_out,
     hid, wb, kh0, kh1, vh0, vh1, doh, qh, qacc, qs, hs, ht, ck, cv, dks, dvs, atth, dqg, dqc, pw, r1, r1s, r2,
-    dhs, dhr, dho, idg, ids_s, ssem, rsem,
+    dhs, dhr, dho, idv, idg, ids_s, ssem, rsem,
 ):
     dp = lax.axis_index("dp")
     seq = lax.axis_index("seq")
@@ -79,6 +79,9 @@
 
     sibling = peer(0, 1)
     others = [(dy, dc) for dy in (1, 3, 2, 0) for dc in (0, 1) if (dy, dc) != (0, 0)]
+
+    idv[...] = jnp.zeros_like(idv)
+    idv[0:2, 0:2] = ids[...]
 
     own_w = local(weight.at[:, pl.ds(pl.multiple_of(half, 1024), 1024)], wb.at[dp], 0)
     own_hid = local(hidden, hid.at[pl.ds(pl.multiple_of(c * 128, 128), 128)], 1)
@@ -157,7 +160,7 @@
             go(w_copy(t, 2, 0, slot))
 
     for j, (dy, dc) in enumerate(others):
-        go(remote(ids, idg.at[seq], S_ID + j, (dp, peer(dy, dc))))
+        go(remote(idv, idg.at[seq], S_ID + j, (dp, peer(dy, dc))))
     own_hid.wait()
     own_hid_rows = hid.at[pl.ds(pl.multiple_of(c * 128, 128), 128)]
     hid_copy = remote(own_hid_rows, own_hid_rows, S_HID, (dp, sibling))
@@ -258,8 +261,8 @@
 
     for j, (dy, dc) in enumerate(others):
         frm = peer(-dy, -dc + 2)
-        remote(ids, idg.at[frm], S_ID + j, (dp, frm)).wait_recv()
-    idg[seq] = ids[...]
+        remote(idv, idg.at[frm], S_ID + j, (dp, frm)).wait_recv()
+    idg[seq] = idv[...]
     to_smem = local(idg, ids_s, 7)
     to_smem.start()
     to_smem.wait()
@@ -294,7 +297,7 @@
         def _(s):
             for u in range(2):
                 rows = pl.ds(pl.multiple_of(s * 128 + u * BLOCK, BLOCK), BLOCK)
-                first, second = ids_s[s, 0, 2 * u], ids_s[s, 0, 2 * u + 1]
+                first, second = ids_s[s, u, 0], ids_s[s, u, 1]
                 k = jnp.concatenate([kh[h][first], kh[h][second]], axis=0)
                 v = jnp.concatenate([vh[h][first], vh[h][second]], axis=0)
                 q = qh[rows, lanes]
@@ -348,7 +351,7 @@
                 for s in range(8):
                     at = jnp.int32(32)
                     for j in range(4):
-                        at = jnp.where(ids_s[s, 0, j] == row, 4 * s + j, at)
+                        at = jnp.where(ids_s[s, j // 2, j % 2] == row, 4 * s + j, at)
                     total_k += ck[at].astype(F32)
                     total_v += cv[at].astype(F32)
                 dks[h, row] = total_k.astype(BF16)
@@ -540,16 +543,40 @@
         copy.wait_send()
 
 
-def finish(att_in, dh_in, dwq_in, dk_in, dv_in, att_out, dh_out, dwq_out, dk_out, dv_out):
-    att_out[...] = att_in[...]
-    dh_out[...] = dh_in[...]
-    dwq_out[...] = dwq_in[...]
-    dk_out[...] = dk_in[...].astype(F32)
-    dv_out[...] = dv_in[...].astype(F32)
+FINISH_PARTS = 4
+
+
+def finish(
+    att_in, dh_in, dwq_in, dk_in, dv_in, att_out, dh_out, dwq_out, dk_out, dv_out,
+    att, dh, dwq, dk, dv, dk_wide, dv_wide, in_sem, out_sem,
+):
+    rows = 512 // FINISH_PARTS
+    loads, stores = [], []
+    for k in range(FINISH_PARTS):
+        span = pl.ds(k * rows, rows)
+        for t, (src, dst) in enumerate(((dk_in, dk), (dv_in, dv))):
+            loads.append(pltpu.make_async_copy(src.at[span], dst.at[span], in_sem.at[2 * k + t]))
+    small = ((att_in, att, att_out), (dh_in, dh, dh_out), (dwq_in, dwq, dwq_out))
+    for t, (src, mid, _) in enumerate(small):
+        loads.append(pltpu.make_async_copy(src, mid, in_sem.at[2 * FINISH_PARTS + t]))
+    for load in loads:
+        load.start()
+    for k in range(FINISH_PARTS):
+        span = pl.ds(k * rows, rows)
+        for t, (narrow, wide, dst) in enumerate(((dk, dk_wide, dk_out), (dv, dv_wide, dv_out))):
+            loads[2 * k + t].wait()
+            wide[span, :] = narrow[span, :].astype(F32)
+            stores.append(pltpu.make_async_copy(wide.at[span], dst.at[span], out_sem.at[2 * k + t]))
+            stores[-1].start()
+    for t, (_, mid, dst) in enumerate(small):
+        loads[2 * FINISH_PARTS + t].wait()
+        stores.append(pltpu.make_async_copy(mid, dst, out_sem.at[2 * FINISH_PARTS + t]))
+        stores[-1].start()
+    for store in stores:
+        store.wait()
 
 
 def on_device(hidden, w_query, nbr_keys, nbr_values, nbr_ids, d_attended):
-    ids = jnp.pad(nbr_ids.reshape(1, 4), ((0, 7), (0, 124)))
     vmem = pltpu.VMEM
     anywhere = pl.BlockSpec(memory_space=pl.ANY)
     in_vmem = pl.BlockSpec(memory_space=pltpu.VMEM)
@@ -588,6 +615,7 @@
             vmem((128, 4096), F32),
             vmem((128, 4096), F32),
             vmem((128, 4096), F32),
+            vmem((8, 128), jnp.int32),
             vmem((8, 8, 128), jnp.int32),
             pltpu.SMEM((8, 8, 128), jnp.int32),
             pltpu.SemaphoreType.DMA((N_SEMS,)),
@@ -597,17 +625,19 @@
             collective_id=0, has_side_effects=True, vmem_limit_bytes=60 * 2**20
         ),
         name="group_attention",
-    )(hidden, w_query, nbr_keys, nbr_values, ids, d_attended)
+    )(hidden, w_query, nbr_keys, nbr_values, nbr_ids, d_attended)
     parts = (attended, d_hidden, d_wq, d_keys.reshape(512, 2048), d_values.reshape(512, 2048))
-    steps = 8
-    specs = [pl.BlockSpec((p.shape[0] // steps, p.shape[1]), lambda i: (i, 0)) for p in parts]
     kinds = (BF16, BF16, F32, F32, F32)
     attended, d_hidden, d_wq, d_keys, d_values = pl.pallas_call(
         finish,
-        grid=(steps,),
         out_shape=[jax.ShapeDtypeStruct(p.shape, kind) for p, kind in zip(parts, kinds)],
-        in_specs=specs,
-        out_specs=specs,
+        in_specs=[anywhere] * 5,
+        out_specs=[anywhere] * 5,
+        scratch_shapes=[
+            *[vmem(p.shape, p.dtype) for p in parts],
+            *[vmem((512, 2048), F32)] * 2,
+            *[pltpu.SemaphoreType.DMA((2 * FINISH_PARTS + 3,))] * 2,
+        ],
         compiler_params=pltpu.CompilerParams(vmem_limit_bytes=60 * 2**20),
         name="finish",
     )(*parts)

time: 163 us -> 159 us (0.975)
  Pallas kernels: 159 us -> 156 us
    pallas_call x1, Pallas kernels: 8.3 us -> 5.36 us  [on_device(): pl.pallas_call(finish, out_shape=[jax.ShapeDtypeStruct(p.shape, kind) for...]
where the time goes in v3:
time: 159 us; the launch traced here: 157 us
  Pallas kernels  156 us (98%)
    pallas_call x1, Pallas kernels, on_device(): pl.pallas_call(kernel, out_shape=(jax.ShapeDtypeStruct((128, 2048), BF16)...  151 us
    pallas_call x1, Pallas kernels, on_device(): pl.pallas_call(finish, out_shape=[jax.ShapeDtypeStruct(p.shape, kind) for...  5.36 us

profile of v3, /device:TPU:1, one launch (start us, length us, event | category | flops | bytes accessed | tf_op | source)
XLA Modules:
  0.0 156.6 jit_solution(18293346164416661647)
XLA Ops:
  0.6 150.6 %group_attention.1 = (bf16[128,2048]{1,0:T(8,128)(2,1)}, bf16[128,4096]{1,0:T(8,128)(2,1)}, f32[512,128]{1,0:T(8,128)}, bf16[4,128,2048]{2,1,0:T(8,128)(2,1)}, bf16[4,128,2048]{2,1,0:T(8,128)(2,1)}) custom-call(bf16[128,4096]{1,0:T(8,128)(2,1)} %hidden.1, bf16[256,2048]{1,0:T(8,128)(2,1)} %weight.1, bf16[4,128,2048]{2,1,0:T(8,128)(2,1)} %keys.1, ...), custom_call_target="tpu_custom_call" | custom-call | tf_op jit(solution)/shard_map/group_attention/pallas_call | solution.py:583
  151.2 5.4 %finish.1 = (bf16[128,2048]{1,0:T(8,128)(2,1)}, bf16[128,4096]{1,0:T(8,128)(2,1)}, f32[512,128]{1,0:T(8,128)}, f32[512,2048]{1,0:T(8,128)}, f32[512,2048]{1,0:T(8,128)}) custom-call(bf16[128,2048]{1,0:T(8,128)(2,1)} %get-tuple-element.15.att_in, bf16[128,4096]{1,0:T(8,128)(2,1)} %get-tuple-element.16.dh_in, f32[512,128]{1,0:T(8,128)} %get-tuple-element.17.dwq_in, ...), custom_call_target="tpu_custom_call" | custom-call | tf_op jit(solution)/shard_map/finish/pallas_call | solution.py:631

commit v4 on v0

v4 whole, which is shorter than its diff:
```python
import functools

import jax
import jax.numpy as jnp
from jax import lax
from jax.experimental import pallas as pl
from jax.experimental.pallas import tpu as pltpu
from jax.sharding import PartitionSpec as P

BF16 = jnp.bfloat16
F32 = jnp.float32
MESH = pl.DeviceIdType.MESH
HEAD = 128
SCALE = HEAD ** (-0.5)
BLOCK = 64
NLEN = 128


class Pool:
    def __init__(self):
        self.used = 0

    def take(self, count):
        first = self.used
        self.used += count
        return first


POOL = Pool()
S_W = POOL.take(80)
S_KV = POOL.take(4)
S_DO = POOL.take(1)
S_GG = POOL.take(4)
S_ID = POOL.take(8)
S_HID = POOL.take(1)
S_Q = POOL.take(8)
S_HS = POOL.take(4)
S_HF = POOL.take(4)
S_ST = POOL.take(8)
S_RET = POOL.take(16)
S_DQ = POOL.take(8)
S_DKV = POOL.take(2)
S_ATT = POOL.take(1)
S_DH = POOL.take(1)
S_R1 = POOL.take(16)
S_R2 = POOL.take(4)
S_LOCAL = POOL.take(16)
N_SEMS = POOL.used
SLOTS = 16


def dot(a, b, dims=((1,), (0,))):
    return lax.dot_general(a, b, (dims, ((), ())), preferred_element_type=F32)


def kernel(
    hidden, weight, keys, values, ids, grads,
    att_out, dh_out, dwq_out, dk_out, dv_out,
    hid, wb0, wb1, kc0, kc1, vc0, vc1, gg, qg0, qg1, qacc, hs, ht, st_buf, dp_buf, low_buf, ds_buf, stat0, stat1,
    sa0, sa1, sd0, sd1, ra0, ra1, rd0, rd1, ck, cv, dks, dvs, att_s, dqg0, dqg1,
    r1, r1s, r2, dhs, dho, dhr, idv, idg, ids_s, ssem, rsem,
):
    dp = lax.axis_index("dp")
    seq = lax.axis_index("seq")
    x, z = dp // 4, dp % 4
    y, c = seq // 2, seq % 2
    wb, kc, vc, qg, stat = (wb0, wb1), (kc0, kc1), (vc0, vc1), (qg0, qg1), (stat0, stat1)
    sa, sd, ra, rd, dqg = (sa0, sa1), (sd0, sd1), (ra0, ra1), (rd0, rd1), (dqg0, dqg1)

    def remote(src, dst, sem, to):
        return pltpu.make_async_remote_copy(
            src_ref=src, dst_ref=dst, send_sem=ssem.at[sem], recv_sem=rsem.at[sem],
            device_id=to, device_id_type=MESH,
        )

    def local(src, dst, sem):
        return pltpu.make_async_copy(src, dst, ssem.at[S_LOCAL + sem])

    def peer(dy, dc):
        return ((y + dy + 4) % 4) * 2 + (c + dc) % 2

    def wide(core):
        return pl.ds(pl.multiple_of(core * 1024, 1024), 1024)

    def chunk(core, ch):
        return pl.ds(pl.multiple_of(core * 1024 + ch * 512, 512), 512)

    sibling = peer(0, 1)
    others = [(dy, dc) for dy in (1, 3, 2, 0) for dc in (0, 1) if (dy, dc) != (0, 0)]

    idv[...] = jnp.zeros_like(idv)
    idv[0:2, 0:2] = ids[...]

    own_w = [local(weight.at[:, chunk(c, ch)], wb[ch].at[dp], ch) for ch in range(2)]
    own_hid = local(hidden, hid.at[pl.ds(pl.multiple_of(c * 128, 128), 128)], 2)
    own_blocks = pl.ds(4 * y + 2 * c, 2)
    own_do = local(grads.at[:, :, wide(c)], gg.at[own_blocks], 3)
    own_rows = pl.ds(4 * c, 4)
    own_kv = [
        local(src.at[:, :, chunk(c, ch)], dst[ch].at[own_rows], 4 + 2 * i + ch)
        for i, (src, dst) in enumerate(((keys, kc), (values, vc))) for ch in range(2)
    ]
    for copy in own_w + [own_hid, own_do] + own_kv:
        copy.start()

    barrier = pltpu.get_barrier_semaphore()

    def greet(to):
        pl.semaphore_signal(barrier, inc=1, device_id=to, device_id_type=MESH)

    for dy, dc in others:
        greet((dp, peer(dy, dc)))
    for step in (1, 2, 3):
        for core in (0, 1):
            greet((((x + step) % 4) * 4 + z, y * 2 + core))
            greet((x * 4 + (z + step) % 4, y * 2 + core))
    pl.semaphore_wait(barrier, 7 + 12)

    def moved(axis, step):
        if axis == 0:
            return (((x + step + 4) % 4) * 4 + z, seq)
        return (x * 4 + (z + step + 4) % 4, seq)

    def source(t, r1_, r2_):
        rx, rz = (r1_, r2_) if t == 0 else (r2_, r1_)
        return ((x + rx + 4) % 4) * 4 + (z + rz + 4) % 4

    LINE = (0, -1, 1, 2)
    PART = {"all": (0, 128), "lo": (0, 64), "hi": (64, 64)}

    def piece(ch, t, r1_, r2_, part):
        lo, n = PART[part]
        return wb[ch].at[source(t, r1_, r2_), pl.ds(t * 128 + lo, n)]

    def w_parts(ch, t, phase, q, slot):
        axis = t if phase == 1 else 1 - t
        sem = S_W + 40 * ch + 20 * t + (slot if phase == 1 else 4 + 4 * q + slot)
        step = 1 if slot % 2 == 0 else -1
        return axis, sem, step, "all" if slot < 2 else ("lo" if slot == 2 else "hi")

    def w_copy(ch, t, phase, q, slot):
        axis, sem, step, part = w_parts(ch, t, phase, q, slot)
        near = 0 if slot < 2 else -step
        src = piece(ch, t, near, 0, part) if phase == 1 else piece(ch, t, LINE[q], near, part)
        return remote(src, src, sem, moved(axis, step))

    def w_recv(ch, t, phase, q, slot):
        axis, sem, step, part = w_parts(ch, t, phase, q, slot)
        far = -step if slot < 2 else 2
        dst = piece(ch, t, far, 0, part) if phase == 1 else piece(ch, t, LINE[q], far, part)
        remote(dst, dst, sem, moved(axis, step)).wait_recv()

    sent = []

    def go(copy):
        copy.start()
        sent.append(copy)

    def w_wave(ch, wave):
        if wave == 0:
            own_w[ch].wait()
            for phase in (1, 2):
                for t in (0, 1):
                    for slot in (0, 1):
                        go(w_copy(ch, t, phase, 0, slot))
        elif wave == 1:
            for t in (0, 1):
                for slot, q in ((0, 1), (1, 2)):
                    w_recv(ch, t, 1, 0, slot)
                    go(w_copy(ch, t, 1, 0, slot + 2))
                    for s in (0, 1):
                        go(w_copy(ch, t, 2, q, s))
        elif wave == 3:
            for t in (0, 1):
                for slot in (2, 3):
                    w_recv(ch, t, 1, 0, slot)
                for s in (0, 1):
                    go(w_copy(ch, t, 2, 3, s))
        else:
            for q in {2: (0,), 4: (1, 2), 5: (3,)}[wave]:
                for t in (0, 1):
                    for slot in (0, 1):
                        w_recv(ch, t, 2, q, slot)
                        go(w_copy(ch, t, 2, q, slot + 2))

    def ring_copy(ref, sem, slot):
        step = 1 if slot % 2 == 0 else -1
        near = y if slot < 2 else (y - step + 4) % 4
        lo, n = ((0, 4), (0, 4), (0, 2), (2, 2))[slot]
        part = ref.at[pl.ds(4 * near + lo, n)]
        return remote(part, part, sem + slot, (dp, peer(step, 0)))

    def ring_recv(ref, sem, slot):
        step = 1 if slot % 2 == 0 else -1
        far = (y - step + 4) % 4 if slot < 2 else (y + 2) % 4
        lo, n = ((0, 4), (0, 4), (0, 2), (2, 2))[slot]
        part = ref.at[pl.ds(4 * far + lo, n)]
        remote(part, part, sem + slot, (dp, peer(step, 0))).wait_recv()

    def ring_send(ref, sem):
        for slot in (0, 1):
            go(ring_copy(ref, sem, slot))

    def ring_forward(ref, sem):
        for slot in (0, 1):
            ring_recv(ref, sem, slot)
            go(ring_copy(ref, sem, slot + 2))

    def ring_finish(ref, sem):
        for slot in (2, 3):
            ring_recv(ref, sem, slot)

    def project(ch, rx):
        @pl.loop(0, 4)
        def _(i):
            d = ((x + rx + 4) % 4) * 4 + i
            rows = hid[:, pl.ds(pl.multiple_of(d * 256, 256), 256)]
            for n in range(2):
                span = slice(n * 256, n * 256 + 256)
                qacc[:, span] += dot(rows, wb[ch][d, :, span])

    def query(ch):
        qacc[...] = jnp.zeros_like(qacc)
        for q, rx in ((0, 0), (1, -1), (2, 1)):
            for slot in (2, 3):
                w_recv(ch, 0, 2, q, slot)
            project(ch, rx)
        for slot in (2, 3):
            w_recv(ch, 0, 2, 3, slot)
            for q in range(4):
                w_recv(ch, 1, 2, q, slot)
        project(ch, 2)
        qg[ch][pl.ds(4 * y, 4)] = qacc[...].astype(BF16).reshape(4, BLOCK, 512)
        ring_send(qg[ch], S_Q + 4 * ch)

    def span256(k):
        return pl.ds(pl.multiple_of(k * 256, 256), 256)

    def feats(k):
        return pl.ds(pl.multiple_of(k * 1024, 1024), 1024)

    def tokens(s):
        return pl.ds(pl.multiple_of(s * 128, 128), 128)

    own_hid_rows = hid.at[tokens(c)]
    hidden_out = []

    def send_hidden():
        for dy in (1, 3, 2):
            to = peer(dy, 0)
            go(remote(own_hid_rows.at[:, feats(to // 2)], hs.at[tokens(seq)], S_HS + dy, (dp, to)))
        hs[span256(y), :] = hid[:, feats(y)]

    def forward_hidden():
        for dy in (1, 3, 2):
            frm = peer(-dy, 0)
            ref = hs.at[tokens(frm)]
            remote(ref, ref, S_HS + dy, (dp, frm)).wait_recv()
            hidden_out.append(remote(ref, ref, S_HF + dy, (dp, sibling)))
            hidden_out[-1].start()

    def slot_of(s, core):
        shard = 2 * y + core
        block, row, other = jnp.int32(0), jnp.int32(0), jnp.int32(0)
        for j in range(4):
            here = ids_s[s, j // 2, j % 2]
            hit = here // 4 == shard
            block = jnp.where(hit, j // 2, block)
            row = jnp.where(hit, here % 4, row)
            other = jnp.where(hit, ids_s[s, j // 2, 1 - j % 2], other)
        return 2 * s + block, 4 * core + row, other

    def diagonal(a, b):
        none = jnp.zeros((BLOCK, HEAD), BF16)
        return jnp.concatenate(
            [jnp.concatenate([a, none], axis=1), jnp.concatenate([none, b], axis=1)], axis=0
        )

    def operands(ch, e, b0, k0, b1, k1):
        lanes = slice(e * HEAD, e * HEAD + HEAD)
        far = slice(ch * 512 + e * HEAD, ch * 512 + e * HEAD + HEAD)
        kk = jnp.concatenate([kc[ch][k0, :, lanes], kc[ch][k1, :, lanes]], axis=1)
        vv = jnp.concatenate([vc[ch][k0, :, lanes], vc[ch][k1, :, lanes]], axis=1)
        qq = diagonal(qg[ch][b0, :, lanes], qg[ch][b1, :, lanes])
        dd = diagonal(gg[b0, :, far], gg[b1, :, far])
        return lanes, kk, vv, qq, dd

    def first_pass(ch):
        @pl.loop(0, 8)
        def _(s):
            b0, k0, _o0 = slot_of(s, 0)
            b1, k1, _o1 = slot_of(s, 1)
            for e in range(4):
                _, kk, vv, qq, dd = operands(ch, e, b0, k0, b1, k1)
                scores = dot(kk, qq, ((1,), (1,))) * SCALE
                d_probs = dot(vv, dd, ((1,), (1,)))
                peak = jnp.max(scores, axis=0, keepdims=True)
                expo = jnp.exp(scores - peak)
                total = jnp.sum(expo, axis=0, keepdims=True)
                st_buf[4 * s + e] = scores
                dp_buf[4 * s + e] = d_probs
                stat[ch][y, s, e:e + 1] = peak + jnp.log(total)
                stat[ch][y, s, 4 + e:5 + e] = jnp.sum(expo * d_probs, axis=0, keepdims=True) / total
        for dy in (1, 3, 2):
            go(remote(stat[ch].at[y], stat[ch].at[y], S_ST + 4 * ch + dy, (dp, peer(dy, 0))))

    def wait_stats(ch):
        for dy in (1, 3, 2):
            frm = peer(-dy, 0)
            ref = stat[ch].at[frm // 2]
            remote(ref, ref, S_ST + 4 * ch + dy, (dp, frm)).wait_recv()

    def second_pass(ch):
        left = lax.broadcasted_iota(jnp.int32, (8, 128), 1) < BLOCK

        @pl.loop(0, 8)
        def _(s):
            b0, k0, o0 = slot_of(s, 0)
            b1, k1, o1 = slot_of(s, 1)
            theirs0 = stat[ch][o0 // 8, s]
            theirs1 = stat[ch][o1 // 8, s]
            turned0 = jnp.concatenate([theirs0[:, BLOCK:], theirs0[:, :BLOCK]], axis=1)
            turned1 = jnp.concatenate([theirs1[:, BLOCK:], theirs1[:, :BLOCK]], axis=1)
            theirs0 = jnp.where((o0 // 4) % 2 == 0, theirs0, turned0)
            theirs1 = jnp.where((o1 // 4) % 2 == 1, theirs1, turned1)
            theirs = jnp.where(left, theirs0, theirs1)
            ours = stat[ch][y, s]
            top = jnp.maximum(ours[:4], theirs[:4])
            whole = top + jnp.log(jnp.exp(ours[:4] - top) + jnp.exp(theirs[:4] - top))
            delta = jnp.exp(ours[:4] - whole) * ours[4:] + jnp.exp(theirs[:4] - whole) * theirs[4:]
            for e in range(4):
                lanes, kk, _, _, _ = operands(ch, e, b0, k0, b1, k1)
                probs = jnp.exp(st_buf[4 * s + e] - whole[e:e + 1])
                low = probs.astype(BF16)
                d_scores = (probs * (dp_buf[4 * s + e] - delta[e:e + 1]) * SCALE).astype(BF16)
                dq = dot(d_scores, kk, ((0,), (0,))).astype(BF16)
                sd[ch][2 * s, :, lanes] = dq[:BLOCK, :HEAD]
                sd[ch][2 * s + 1, :, lanes] = dq[BLOCK:, HEAD:]
                low_buf[4 * s + e] = low
                ds_buf[4 * s + e] = d_scores

    def third_pass(ch):
        @pl.loop(0, 8)
        def _(s):
            b0, k0, _o0 = slot_of(s, 0)
            b1, k1, _o1 = slot_of(s, 1)
            for e in range(4):
                lanes, _, vv, qq, dd = operands(ch, e, b0, k0, b1, k1)
                low, d_scores = low_buf[4 * s + e], ds_buf[4 * s + e]
                att = dot(low, vv, ((0,), (0,))).astype(BF16)
                sa[ch][2 * s, :, lanes] = att[:BLOCK, :HEAD]
                sa[ch][2 * s + 1, :, lanes] = att[BLOCK:, HEAD:]
                dk = dot(d_scores, qq).astype(BF16)
                dv = dot(low, dd).astype(BF16)
                for i in range(2):
                    ck[2 * s + i, :, lanes] = dk[:, i * HEAD:(i + 1) * HEAD]
                    cv[2 * s + i, :, lanes] = dv[:, i * HEAD:(i + 1) * HEAD]

    def give_back(ch, kind):
        src, dst = ((sd, rd), (sa, ra))[kind]
        for dy in (1, 3, 2):
            to = peer(dy, 0)
            go(remote(
                src[ch].at[pl.ds(4 * (to // 2), 4)], dst[ch].at[pl.ds(4 * y, 4)],
                S_RET + 8 * kind + 4 * ch + dy, (dp, to),
            ))
        dst[ch][pl.ds(4 * y, 4)] = src[ch][pl.ds(4 * y, 4)]

    def take_back(ch, kind):
        src, dst = ((sd, rd), (sa, ra))[kind]
        for dy in (1, 3, 2):
            frm = peer(-dy, 0)
            ref = dst[ch].at[pl.ds(4 * (frm // 2), 4)]
            remote(ref, ref, S_RET + 8 * kind + 4 * ch + dy, (dp, frm)).wait_recv()
        for block in range(4):
            core, u = block // 2, block % 2
            total = jnp.zeros((BLOCK, 512), F32)
            for j in range(2):
                name = ids_s[2 * y + core, u, j]
                total += dst[ch][(name // 8) * 4 + core * 2 + (name // 4) % 2].astype(F32)
            if kind == 0:
                dqg[ch][4 * y + block] = total.astype(BF16)
            else:
                att_s[block * BLOCK:(block + 1) * BLOCK, ch * 512:(ch + 1) * 512] = total.astype(BF16)

    def sum_kv(ch):
        @pl.loop(0, 8)
        def _(row):
            at = []
            for s in range(8):
                one = jnp.int32(SLOTS)
                for j in range(4):
                    one = jnp.where(ids_s[s, j // 2, j % 2] == 8 * y + row, 2 * s + row // 4, one)
                at.append(one)
            for src, dst in ((ck, dks), (cv, dvs)):
                for e in range(4):
                    lanes = slice(e * HEAD, e * HEAD + HEAD)
                    total = src[at[0], :, lanes].astype(F32)
                    for s in range(1, 8):
                        total += src[at[s], :, lanes].astype(F32)
                    dst[row, :, ch * 512 + e * HEAD:ch * 512 + (e + 1) * HEAD] = total.astype(BF16)

    def wq_grad(k):
        ch, pair = k // 2, k % 2
        both = dqg[ch][:, :, pair * 256:pair * 256 + 256].reshape(1024, 256)
        for m in range(4):
            hs[m * 256:m * 256 + 256, k * 256:k * 256 + 256] = dot(
                ht[m * 256:m * 256 + 256, :], both
            ).astype(BF16)

    def r1_copy(core, ch, b):
        src = hs.at[pl.ds(core * 512, 512), pl.ds((4 * ch + b) * HEAD, HEAD)]
        if core == 0:
            slot, part, dest = x, b, (2 * c + ch) * 4 + z
        else:
            slot, part, dest = z, 2 * c + ch, x * 4 + b
        dst = r1.at[slot, part]
        sem = ssem.at[S_R1 + core * 8 + ch * 4 + b]
        own = jnp.logical_and(dest == dp, c == core)
        return src, dst, sem, rsem.at[S_R1 + slot * 4 + part], (dest, y * 2 + core), own

    def r1_start(core, ch, b):
        src, dst, s_sem, r_sem, dest, own = r1_copy(core, ch, b)

        @pl.when(own)
        def _():
            pltpu.make_async_copy(src, dst, s_sem).start()

        @pl.when(jnp.logical_not(own))
        def _():
            pltpu.make_async_remote_copy(
                src_ref=src, dst_ref=dst, send_sem=s_sem, recv_sem=r_sem, device_id=dest, device_id_type=MESH
            ).start()

    def r1_wait(core, ch, b):
        src, dst, s_sem, r_sem, dest, own = r1_copy(core, ch, b)

        @pl.when(own)
        def _():
            pltpu.make_async_copy(src, dst, s_sem).wait()

        @pl.when(jnp.logical_not(own))
        def _():
            pltpu.make_async_remote_copy(
                src_ref=src, dst_ref=dst, send_sem=s_sem, recv_sem=r_sem, device_id=dest, device_id_type=MESH
            ).wait_send()

    def wq_send(k):
        wq_grad(k)
        for b in (2 * (k % 2), 2 * (k % 2) + 1):
            for core in range(2):
                r1_start(core, k // 2, b)

    w_wave(0, 0)
    own_hid.wait()
    go(remote(own_hid_rows, own_hid_rows, S_HID, (dp, sibling)))
    go(remote(grads.at[:, :, wide(1 - c)], gg.at[own_blocks], S_DO, (dp, sibling)))
    for j, (dy, dc) in enumerate(others):
        go(remote(idv, idg.at[seq], S_ID + j, (dp, peer(dy, dc))))
    for i, (src, dst) in enumerate(((keys, kc), (values, vc))):
        for ch in range(2):
            go(remote(src.at[:, :, chunk(1 - c, ch)], dst[ch].at[own_rows], S_KV + 2 * i + ch, (dp, sibling)))
    w_wave(0, 1)
    their_blocks = gg.at[pl.ds(4 * y + 2 * (1 - c), 2)]
    remote(their_blocks, their_blocks, S_DO, (dp, sibling)).wait_recv()
    own_do.wait()
    ring_send(gg, S_GG)
    w_wave(0, 2)
    w_wave(0, 3)
    w_wave(1, 0)
    other_rows = hid.at[tokens(1 - c)]
    remote(other_rows, other_rows, S_HID, (dp, sibling)).wait_recv()
    w_wave(0, 4)
    ring_forward(gg, S_GG)
    w_wave(0, 5)
    for j, (dy, dc) in enumerate(others):
        frm = peer(-dy, -dc + 2)
        remote(idv, idg.at[frm], S_ID + j, (dp, frm)).wait_recv()
    idg[seq] = idv[...]
    to_smem = local(idg, ids_s, 8)
    to_smem.start()
    to_smem.wait()
    query(0)
    w_wave(1, 1)
    w_wave(1, 2)
    ck[SLOTS] = jnp.zeros((NLEN, 512), BF16)
    cv[SLOTS] = jnp.zeros((NLEN, 512), BF16)
    for copy in own_kv:
        copy.wait()
    their_rows = pl.ds(4 * (1 - c), 4)
    for i, dst in enumerate((kc, vc)):
        for ch in range(2):
            ref = dst[ch].at[their_rows]
            remote(ref, ref, S_KV + 2 * i + ch, (dp, sibling)).wait_recv()
    ring_forward(qg[0], S_Q)
    send_hidden()
    w_wave(1, 3)
    w_wave(1, 4)
    ring_finish(gg, S_GG)
    ring_finish(qg[0], S_Q)
    first_pass(0)
    w_wave(1, 5)
    def dh_add(ch, first):
        @pl.loop(0, 16)
        def _(d):
            for core, buf in ((1 - c, dhs), (c, dho)):
                rows = dqg[ch][pl.ds(4 * y + 2 * core, 2)].reshape(128, 512)
                part = dot(rows, wb[ch][d], ((1,), (1,)))
                if first:
                    buf[:, span256(d)] = part
                else:
                    buf[:, span256(d)] += part

    query(1)
    wait_stats(0)
    second_pass(0)
    ring_forward(qg[1], S_Q + 4)
    give_back(0, 0)
    third_pass(0)
    sum_kv(0)
    ring_finish(qg[1], S_Q + 4)
    first_pass(1)
    take_back(0, 0)
    ring_send(dqg[0], S_DQ)
    wait_stats(1)
    second_pass(1)
    give_back(1, 0)
    forward_hidden()
    ring_forward(dqg[0], S_DQ)
    third_pass(1)
    for dy in (1, 3, 2):
        frm = peer(-dy, 1)
        ref = hs.at[tokens(frm)]
        remote(ref, ref, S_HF + dy, (dp, sibling)).wait_recv()

    @pl.loop(0, 4)
    def _(m):
        ht[span256(m), :] = jnp.transpose(hs[:, span256(m)])

    for copy in hidden_out:
        copy.wait_send()
    dh_add(0, True)
    take_back(1, 0)
    ring_send(dqg[1], S_DQ + 4)
    ring_finish(dqg[0], S_DQ)
    wq_send(0)
    ring_forward(dqg[1], S_DQ + 4)
    give_back(0, 1)
    give_back(1, 1)
    wq_send(1)
    sum_kv(1)
    their_kv = []
    for i, (src, dst) in enumerate(((dks, dk_out), (dvs, dv_out))):
        go(remote(src.at[their_rows], dst.at[:, :, wide(c)], S_DKV + i, (dp, sibling)))
        their_kv.append(remote(src.at[their_rows], dst.at[:, :, wide(1 - c)], S_DKV + i, (dp, sibling)))
    own_kv_out = [
        local(src.at[own_rows], dst.at[:, :, wide(c)], 9 + i)
        for i, (src, dst) in enumerate(((dks, dk_out), (dvs, dv_out)))
    ]
    for copy in own_kv_out:
        copy.start()
    ring_finish(dqg[1], S_DQ + 4)
    wq_send(2)
    wq_send(3)
    dh_add(1, False)
    dh_copy = remote(dhs, dhr, S_DH, (dp, sibling))
    go(dh_copy)

    for core in range(2):
        for ch in range(2):
            for b in range(4):
                r1_wait(core, ch, b)
    line1, line2 = jnp.where(c == 0, x, z), jnp.where(c == 0, z, x)

    @pl.loop(0, 16)
    def _(k):
        from_core = jnp.where(c == 0, x // 2, (k % 4) // 2)

        @pl.when(jnp.logical_not(jnp.logical_and(k // 4 == line1, from_core == c)))
        def _():
            ref = r1.at[k // 4, k % 4]
            pltpu.make_async_remote_copy(
                src_ref=ref, dst_ref=ref, send_sem=ssem.at[S_R1], recv_sem=rsem.at[S_R1 + k],
                device_id=(dp, sibling), device_id_type=MESH,
            ).wait_recv()

    def r2_copy(step):
        to = (line2 + step) % 4
        dest = jnp.where(c == 0, line1 * 4 + to, to * 4 + line1)
        return remote(r1s.at[to], r2.at[step], S_R2 + step, (dest, seq))

    for step in (1, 3, 2, 0):
        to = (line2 + step) % 4
        total = r1[0, to].astype(F32)
        for k in range(1, 4):
            total += r1[k, to].astype(F32)
        if step:
            r1s[to] = total.astype(BF16)
            go(r2_copy(step))
        else:
            dwq_out[...] = total
    dh_copy.wait_recv()
    dh_out[...] = (dho[...] + dhr[...]).astype(BF16)
    for step in (1, 3, 2):
        r2_copy(step).wait_recv()
        dwq_out[...] += r2[step].astype(F32)
    for ch in range(2):
        take_back(ch, 1)
    own_att = local(att_s.at[tokens(c)], att_out.at[:, wide(c)], 11)
    own_att.start()
    go(remote(att_s.at[tokens(1 - c)], att_out.at[:, wide(c)], S_ATT, (dp, sibling)))

    own_att.wait()
    remote(att_s.at[tokens(1 - c)], att_out.at[:, wide(1 - c)], S_ATT, (dp, sibling)).wait_recv()
    for copy in own_kv_out:
        copy.wait()
    for copy in their_kv:
        copy.wait_recv()
    for copy in sent:
        copy.wait_send()


FINISH_PARTS = 4


def finish(
    att_in, dh_in, dwq_in, dk_in, dv_in, att_out, dh_out, dwq_out, dk_out, dv_out,
    att, dh, dwq, dk, dv, dk_wide, dv_wide, in_sem, out_sem,
):
    rows = 512 // FINISH_PARTS
    loads, stores = [], []
    for k in range(FINISH_PARTS):
        span = pl.ds(k * rows, rows)
        for t, (src, dst) in enumerate(((dk_in, dk), (dv_in, dv))):
            loads.append(pltpu.make_async_copy(src.at[span], dst.at[span], in_sem.at[2 * k + t]))
    small = ((att_in, att, att_out), (dh_in, dh, dh_out), (dwq_in, dwq, dwq_out))
    for t, (src, mid, _) in enumerate(small):
        loads.append(pltpu.make_async_copy(src, mid, in_sem.at[2 * FINISH_PARTS + t]))
    for load in loads:
        load.start()
    for k in range(FINISH_PARTS):
        span = pl.ds(k * rows, rows)
        for t, (narrow, wide, dst) in enumerate(((dk, dk_wide, dk_out), (dv, dv_wide, dv_out))):
            loads[2 * k + t].wait()
            wide[span, :] = narrow[span, :].astype(F32)
            stores.append(pltpu.make_async_copy(wide.at[span], dst.at[span], out_sem.at[2 * k + t]))
            stores[-1].start()
    for t, (_, mid, dst) in enumerate(small):
        loads[2 * FINISH_PARTS + t].wait()
        stores.append(pltpu.make_async_copy(mid, dst, out_sem.at[2 * FINISH_PARTS + t]))
        stores[-1].start()
    for store in stores:
        store.wait()


def on_device(hidden, w_query, nbr_keys, nbr_values, nbr_ids, d_attended):
    vmem = pltpu.VMEM
    anywhere = pl.BlockSpec(memory_space=pl.ANY)
    in_vmem = pl.BlockSpec(memory_space=pltpu.VMEM)
    attended, d_hidden, d_wq, d_keys, d_values = pl.pallas_call(
        kernel,
        out_shape=(
            jax.ShapeDtypeStruct((128, 2048), BF16),
            jax.ShapeDtypeStruct((128, 4096), BF16),
            jax.ShapeDtypeStruct((512, 128), F32),
            jax.ShapeDtypeStruct((4, 128, 2048), BF16),
            jax.ShapeDtypeStruct((4, 128, 2048), BF16),
        ),
        in_specs=[anywhere, anywhere, anywhere, anywhere, in_vmem, anywhere],
        out_specs=(anywhere, in_vmem, in_vmem, anywhere, anywhere),
        scratch_shapes=[
            vmem((256, 4096), BF16),
            *[vmem((16, 256, 512), BF16)] * 2,
            *[vmem((8, 128, 512), BF16)] * 4,
            vmem((16, 64, 1024), BF16),
            *[vmem((16, 64, 512), BF16)] * 2,
            vmem((256, 512), F32),
            vmem((1024, 1024), BF16),
            vmem((1024, 1024), BF16),
            vmem((32, 128, 128), F32),
            vmem((32, 128, 128), F32),
            vmem((32, 128, 128), BF16),
            vmem((32, 128, 128), BF16),
            *[vmem((4, 8, 8, 128), F32)] * 2,
            *[vmem((SLOTS, 64, 512), BF16)] * 8,
            *[vmem((SLOTS + 1, 128, 512), BF16)] * 2,
            *[vmem((8, 128, 1024), BF16)] * 2,
            vmem((256, 1024), BF16),
            *[vmem((16, 64, 512), BF16)] * 2,
            vmem((4, 4, 512, 128), BF16),
            vmem((4, 512, 128), BF16),
            vmem((4, 512, 128), BF16),
            vmem((128, 4096), F32),
            vmem((128, 4096), F32),
            vmem((128, 4096), F32),
            vmem((8, 128), jnp.int32),
            vmem((8, 8, 128), jnp.int32),
            pltpu.SMEM((8, 8, 128), jnp.int32),
            pltpu.SemaphoreType.DMA((N_SEMS,)),
            pltpu.SemaphoreType.DMA((N_SEMS,)),
        ],
        compiler_params=pltpu.CompilerParams(
            collective_id=0, has_side_effects=True, vmem_limit_bytes=62 * 2**20
        ),
        name="group_attention",
    )(hidden, w_query, nbr_keys, nbr_values, nbr_ids, d_attended.reshape(2, 64, 2048))
    parts = (attended, d_hidden, d_wq, d_keys.reshape(512, 2048), d_values.reshape(512, 2048))
    kinds = (BF16, BF16, F32, F32, F32)
    attended, d_hidden, d_wq, d_keys, d_values = pl.pallas_call(
        finish,
        out_shape=[jax.ShapeDtypeStruct(p.shape, kind) for p, kind in zip(parts, kinds)],
        in_specs=[anywhere] * 5,
        out_specs=[anywhere] * 5,
        scratch_shapes=[
            *[vmem(p.shape, p.dtype) for p in parts],
            *[vmem((512, 2048), F32)] * 2,
            *[pltpu.SemaphoreType.DMA((2 * FINISH_PARTS + 3,))] * 2,
        ],
        compiler_params=pltpu.CompilerParams(vmem_limit_bytes=60 * 2**20),
        name="finish",
    )(*parts)
    return attended, d_hidden, d_wq, d_keys.reshape(4, 128, 2048), d_values.reshape(4, 128, 2048)


def solution(mesh):
    placed = (
        P(("dp", "seq"), None),
        P("dp", None),
        P(("dp", "seq"), None, None),
        P(("dp", "seq"), None, None),
        P(("dp", "seq"), None),
        P(("dp", "seq"), None),
    )
    return jax.shard_map(
        on_device,
        mesh=mesh,
        in_specs=placed,
        out_specs=(
            P(("dp", "seq"), None),
            P(("dp", "seq"), None),
            P("seq", "dp"),
            P(("dp", "seq"), None, None),
            P(("dp", "seq"), None, None),
        ),
        check_vma=False,
    )
```

time: 388 us -> 154 us (0.40)
  the two profiles are of different devices: /device:TPU:1 before, /device:TPU:59 now
where the time goes in v4:
time: 154 us
  Pallas kernels  153 us (99%)
    pallas_call x1, Pallas kernels, on_device(): pl.pallas_call(kernel, out_shape=(jax.ShapeDtypeStruct((128, 2048), BF16)...  148 us
    pallas_call x1, Pallas kernels, on_device(): pl.pallas_call(finish, out_shape=[jax.ShapeDtypeStruct(p.shape, kind) for...  5.36 us

profile of v4, /device:TPU:59, one launch (start us, length us, event | category | flops | bytes accessed | tf_op | source)
XLA Modules:
  0.0 154.0 jit_solution(2307756725767574531)
XLA Ops:
  0.6 148.0 %group_attention.1 = (bf16[128,2048]{1,0:T(8,128)(2,1)}, bf16[128,4096]{1,0:T(8,128)(2,1)}, f32[512,128]{1,0:T(8,128)}, bf16[4,128,2048]{2,1,0:T(8,128)(2,1)}, bf16[4,128,2048]{2,1,0:T(8,128)(2,1)}) custom-call(bf16[128,4096]{1,0:T(8,128)(2,1)} %hidden.1, bf16[256,2048]{1,0:T(8,128)(2,1)} %weight.1, bf16[4,128,2048]{2,1,0:T(8,128)(2,1)} %keys.1, ...), custom_call_target="tpu_custom_call" | custom-call | tf_op jit(solution)/shard_map/group_attention/pallas_call | solution.py:660
  148.7 5.4 %finish.1 = (bf16[128,2048]{1,0:T(8,128)(2,1)}, bf16[128,4096]{1,0:T(8,128)(2,1)}, f32[512,128]{1,0:T(8,128)}, f32[512,2048]{1,0:T(8,128)}, f32[512,2048]{1,0:T(8,128)}) custom-call(bf16[128,2048]{1,0:T(8,128)(2,1)} %get-tuple-element.15.att_in, bf16[128,4096]{1,0:T(8,128)(2,1)} %get-tuple-element.16.dh_in, f32[512,128]{1,0:T(8,128)} %get-tuple-element.17.dwq_in, ...), custom_call_target="tpu_custom_call" | custom-call | tf_op jit(solution)/shard_map/finish/pallas_call | solution.py:709

commit v5 on v4

--- a/solution.py
+++ b/solution.py
@@ -410,10 +410,7 @@
 
     def r1_copy(core, ch, b):
         src = hs.at[pl.ds(core * 512, 512), pl.ds((4 * ch + b) * HEAD, HEAD)]
-        if core == 0:
-            slot, part, dest = x, b, (2 * c + ch) * 4 + z
-        else:
-            slot, part, dest = z, 2 * c + ch, x * 4 + b
+        slot, part, dest = z, 2 * c + ch, x * 4 + b
         dst = r1.at[slot, part]
         sem = ssem.at[S_R1 + core * 8 + ch * 4 + b]
         own = jnp.logical_and(dest == dp, c == core)
@@ -570,13 +567,10 @@
         for ch in range(2):
             for b in range(4):
                 r1_wait(core, ch, b)
-    line1, line2 = jnp.where(c == 0, x, z), jnp.where(c == 0, z, x)
 
     @pl.loop(0, 16)
     def _(k):
-        from_core = jnp.where(c == 0, x // 2, (k % 4) // 2)
-
-        @pl.when(jnp.logical_not(jnp.logical_and(k // 4 == line1, from_core == c)))
+        @pl.when(jnp.logical_not(jnp.logical_and(k // 4 == z, (k % 4) // 2 == c)))
         def _():
             ref = r1.at[k // 4, k % 4]
             pltpu.make_async_remote_copy(
@@ -585,12 +579,11 @@
             ).wait_recv()
 
     def r2_copy(step):
-        to = (line2 + step) % 4
-        dest = jnp.where(c == 0, line1 * 4 + to, to * 4 + line1)
-        return remote(r1s.at[to], r2.at[step], S_R2 + step, (dest, seq))
+        to = (x + step) % 4
+        return remote(r1s.at[to], r2.at[step], S_R2 + step, (to * 4 + z, seq))
 
     for step in (1, 3, 2, 0):
-        to = (line2 + step) % 4
+        to = (x + step) % 4
         total = r1[0, to].astype(F32)
         for k in range(1, 4):
             total += r1[k, to].astype(F32)

time: 154 us -> 153 us (level)
  the two profiles are of different devices: /device:TPU:59 before, /device:TPU:1 now
where the time goes in v5:
time: 153 us; the launch traced here: 152 us
  Pallas kernels  152 us (99%)
    pallas_call x1, Pallas kernels, on_device(): pl.pallas_call(kernel, out_shape=(jax.ShapeDtypeStruct((128, 2048), BF16)...  146 us
    pallas_call x1, Pallas kernels, on_device(): pl.pallas_call(finish, out_shape=[jax.ShapeDtypeStruct(p.shape, kind) for...  5.36 us

profile of v5, /device:TPU:1, one launch (start us, length us, event | category | flops | bytes accessed | tf_op | source)
XLA Modules:
  0.0 152.4 jit_solution(1157834393421398355)
XLA Ops:
  0.6 146.4 %group_attention.1 = (bf16[128,2048]{1,0:T(8,128)(2,1)}, bf16[128,4096]{1,0:T(8,128)(2,1)}, f32[512,128]{1,0:T(8,128)}, bf16[4,128,2048]{2,1,0:T(8,128)(2,1)}, bf16[4,128,2048]{2,1,0:T(8,128)(2,1)}) custom-call(bf16[128,4096]{1,0:T(8,128)(2,1)} %hidden.1, bf16[256,2048]{1,0:T(8,128)(2,1)} %weight.1, bf16[4,128,2048]{2,1,0:T(8,128)(2,1)} %keys.1, ...), custom_call_target="tpu_custom_call" | custom-call | tf_op jit(solution)/shard_map/group_attention/pallas_call | solution.py:653
  147.0 5.4 %finish.1 = (bf16[128,2048]{1,0:T(8,128)(2,1)}, bf16[128,4096]{1,0:T(8,128)(2,1)}, f32[512,128]{1,0:T(8,128)}, f32[512,2048]{1,0:T(8,128)}, f32[512,2048]{1,0:T(8,128)}) custom-call(bf16[128,2048]{1,0:T(8,128)(2,1)} %get-tuple-element.15.att_in, bf16[128,4096]{1,0:T(8,128)(2,1)} %get-tuple-element.16.dh_in, f32[512,128]{1,0:T(8,128)} %get-tuple-element.17.dwq_in, ...), custom_call_target="tpu_custom_call" | custom-call | tf_op jit(solution)/shard_map/finish/pallas_call | solution.py:702

commit v6 on v5

--- a/solution.py
+++ b/solution.py
@@ -58,7 +58,7 @@
     att_out, dh_out, dwq_out, dk_out, dv_out,
     hid, wb0, wb1, kc0, kc1, vc0, vc1, gg, qg0, qg1, qacc, hs, ht, st_buf, dp_buf, low_buf, ds_buf, stat0, stat1,
     sa0, sa1, sd0, sd1, ra0, ra1, rd0, rd1, ck, cv, dks, dvs, att_s, dqg0, dqg1,
-    r1, r1s, r2, dhs, dho, dhr, idv, idg, ids_s, ssem, rsem,
+    r1, r1s, r2, dhs, dho, dhr, dh_s, dwq_s, idv, idg, ids_s, ssem, rsem,
 ):
     dp = lax.axis_index("dp")
     seq = lax.axis_index("seq")
@@ -358,7 +358,7 @@
 
     def give_back(ch, kind):
         src, dst = ((sd, rd), (sa, ra))[kind]
-        for dy in (1, 3, 2):
+        for dy in (1, 3, 2) if kind == 0 else (2, 1, 3):
             to = peer(dy, 0)
             go(remote(
                 src[ch].at[pl.ds(4 * (to // 2), 4)], dst[ch].at[pl.ds(4 * y, 4)],
@@ -591,19 +591,24 @@
             r1s[to] = total.astype(BF16)
             go(r2_copy(step))
         else:
-            dwq_out[...] = total
+            dwq_s[...] = total
+    take_back(0, 1)
     dh_copy.wait_recv()
-    dh_out[...] = (dho[...] + dhr[...]).astype(BF16)
+    dh_s[...] = (dho[...] + dhr[...]).astype(BF16)
+    late_out = [local(dh_s, dh_out, 12), local(dwq_s, dwq_out, 13)]
+    late_out[0].start()
     for step in (1, 3, 2):
         r2_copy(step).wait_recv()
-        dwq_out[...] += r2[step].astype(F32)
-    for ch in range(2):
-        take_back(ch, 1)
+        dwq_s[...] += r2[step].astype(F32)
+    late_out[1].start()
+    take_back(1, 1)
     own_att = local(att_s.at[tokens(c)], att_out.at[:, wide(c)], 11)
     own_att.start()
     go(remote(att_s.at[tokens(1 - c)], att_out.at[:, wide(c)], S_ATT, (dp, sibling)))
 
     own_att.wait()
+    for copy in late_out:
+        copy.wait()
     remote(att_s.at[tokens(1 - c)], att_out.at[:, wide(1 - c)], S_ATT, (dp, sibling)).wait_recv()
     for copy in own_kv_out:
         copy.wait()
@@ -660,7 +665,7 @@
             jax.ShapeDtypeStruct((4, 128, 2048), BF16),
         ),
         in_specs=[anywhere, anywhere, anywhere, anywhere, in_vmem, anywhere],
-        out_specs=(anywhere, in_vmem, in_vmem, anywhere, anywhere),
+        out_specs=[anywhere] * 5,
         scratch_shapes=[
             vmem((256, 4096), BF16),
             *[vmem((16, 256, 512), BF16)] * 2,
@@ -686,6 +691,8 @@
             vmem((128, 4096), F32),
             vmem((128, 4096), F32),
             vmem((128, 4096), F32),
+            vmem((128, 4096), BF16),
+            vmem((512, 128), F32),
             vmem((8, 128), jnp.int32),
             vmem((8, 8, 128), jnp.int32),
             pltpu.SMEM((8, 8, 128), jnp.int32),

time: 153 us -> 151 us (0.987)
  Pallas kernels: 152 us -> 150 us
    pallas_call x1, Pallas kernels: 146 us -> 145 us  [on_device(): pl.pallas_call(kernel, out_shape=(jax.ShapeDtypeStruct((128, 2048), BF16)...]
where the time goes in v6:
time: 151 us
  Pallas kernels  150 us (99%)
    pallas_call x1, Pallas kernels, on_device(): pl.pallas_call(kernel, out_shape=(jax.ShapeDtypeStruct((128, 2048), BF16)...  145 us
    pallas_call x1, Pallas kernels, on_device(): pl.pallas_call(finish, out_shape=[jax.ShapeDtypeStruct(p.shape, kind) for...  5.36 us

profile of v6, /device:TPU:1, one launch (start us, length us, event | category | flops | bytes accessed | tf_op | source)
XLA Modules:
  0.0 150.7 jit_solution(10277136190411466236)
XLA Ops:
  0.6 144.7 %group_attention.1 = (bf16[128,2048]{1,0:T(8,128)(2,1)}, bf16[128,4096]{1,0:T(8,128)(2,1)}, f32[512,128]{1,0:T(8,128)}, bf16[4,128,2048]{2,1,0:T(8,128)(2,1)}, bf16[4,128,2048]{2,1,0:T(8,128)(2,1)}) custom-call(bf16[128,4096]{1,0:T(8,128)(2,1)} %hidden.1, bf16[256,2048]{1,0:T(8,128)(2,1)} %weight.1, bf16[4,128,2048]{2,1,0:T(8,128)(2,1)} %keys.1, ...), custom_call_target="tpu_custom_call" | custom-call | tf_op jit(solution)/shard_map/group_attention/pallas_call | solution.py:658
  145.3 5.4 %finish.1 = (bf16[128,2048]{1,0:T(8,128)(2,1)}, bf16[128,4096]{1,0:T(8,128)(2,1)}, f32[512,128]{1,0:T(8,128)}, f32[512,2048]{1,0:T(8,128)}, f32[512,2048]{1,0:T(8,128)}) custom-call(bf16[128,2048]{1,0:T(8,128)(2,1)} %get-tuple-element.15.att_in, bf16[128,4096]{1,0:T(8,128)(2,1)} %get-tuple-element.16.dh_in, f32[512,128]{1,0:T(8,128)} %get-tuple-element.17.dwq_in, ...), custom_call_target="tpu_custom_call" | custom-call | tf_op jit(solution)/shard_map/finish/pallas_call | solution.py:709

commit v7 on v6

--- a/solution.py
+++ b/solution.py
@@ -30,15 +30,15 @@
 S_W = POOL.take(80)
 S_KV = POOL.take(4)
 S_DO = POOL.take(1)
-S_GG = POOL.take(4)
+S_GG = POOL.take(6)
 S_ID = POOL.take(8)
 S_HID = POOL.take(1)
-S_Q = POOL.take(8)
+S_Q = POOL.take(12)
 S_HS = POOL.take(4)
 S_HF = POOL.take(4)
 S_ST = POOL.take(8)
 S_RET = POOL.take(16)
-S_DQ = POOL.take(8)
+S_DQ = POOL.take(12)
 S_DKV = POOL.take(2)
 S_ATT = POOL.take(1)
 S_DH = POOL.take(1)
@@ -183,31 +183,31 @@
                         w_recv(ch, t, 2, q, slot)
                         go(w_copy(ch, t, 2, q, slot + 2))
 
+    RING_LO = (0, 2, 2, 0, 0, 2)
+
     def ring_copy(ref, sem, slot):
         step = 1 if slot % 2 == 0 else -1
-        near = y if slot < 2 else (y - step + 4) % 4
-        lo, n = ((0, 4), (0, 4), (0, 2), (2, 2))[slot]
-        part = ref.at[pl.ds(4 * near + lo, n)]
+        near = y if slot < 4 else (y - step + 4) % 4
+        part = ref.at[pl.ds(4 * near + RING_LO[slot], 2)]
         return remote(part, part, sem + slot, (dp, peer(step, 0)))
 
     def ring_recv(ref, sem, slot):
         step = 1 if slot % 2 == 0 else -1
-        far = (y - step + 4) % 4 if slot < 2 else (y + 2) % 4
-        lo, n = ((0, 4), (0, 4), (0, 2), (2, 2))[slot]
-        part = ref.at[pl.ds(4 * far + lo, n)]
+        far = (y - step + 4) % 4 if slot < 4 else (y + 2) % 4
+        part = ref.at[pl.ds(4 * far + RING_LO[slot], 2)]
         remote(part, part, sem + slot, (dp, peer(step, 0))).wait_recv()
 
     def ring_send(ref, sem):
-        for slot in (0, 1):
+        for slot in range(4):
             go(ring_copy(ref, sem, slot))
 
     def ring_forward(ref, sem):
         for slot in (0, 1):
             ring_recv(ref, sem, slot)
-            go(ring_copy(ref, sem, slot + 2))
+            go(ring_copy(ref, sem, slot + 4))
 
     def ring_finish(ref, sem):
-        for slot in (2, 3):
+        for slot in (2, 3, 4, 5):
             ring_recv(ref, sem, slot)
 
     def project(ch, rx):
@@ -231,7 +231,7 @@
                 w_recv(ch, 1, 2, q, slot)
         project(ch, 2)
         qg[ch][pl.ds(4 * y, 4)] = qacc[...].astype(BF16).reshape(4, BLOCK, 512)
-        ring_send(qg[ch], S_Q + 4 * ch)
+        ring_send(qg[ch], S_Q + 6 * ch)
 
     def span256(k):
         return pl.ds(pl.multiple_of(k * 256, 256), 256)
@@ -511,11 +511,11 @@
     query(1)
     wait_stats(0)
     second_pass(0)
-    ring_forward(qg[1], S_Q + 4)
+    ring_forward(qg[1], S_Q + 6)
     give_back(0, 0)
     third_pass(0)
     sum_kv(0)
-    ring_finish(qg[1], S_Q + 4)
+    ring_finish(qg[1], S_Q + 6)
     first_pass(1)
     take_back(0, 0)
     ring_send(dqg[0], S_DQ)
@@ -538,10 +538,10 @@
         copy.wait_send()
     dh_add(0, True)
     take_back(1, 0)
-    ring_send(dqg[1], S_DQ + 4)
+    ring_send(dqg[1], S_DQ + 6)
     ring_finish(dqg[0], S_DQ)
     wq_send(0)
-    ring_forward(dqg[1], S_DQ + 4)
+    ring_forward(dqg[1], S_DQ + 6)
     give_back(0, 1)
     give_back(1, 1)
     wq_send(1)
@@ -556,7 +556,7 @@
     ]
     for copy in own_kv_out:
         copy.start()
-    ring_finish(dqg[1], S_DQ + 4)
+    ring_finish(dqg[1], S_DQ + 6)
     wq_send(2)
     wq_send(3)
     dh_add(1, False)

time: 151 us -> 149 us (0.987)
  Pallas kernels: 150 us -> 148 us
    pallas_call x1, Pallas kernels: 145 us -> 143 us  [on_device(): pl.pallas_call(kernel, out_shape=(jax.ShapeDtypeStruct((128, 2048), BF16)...]
where the time goes in v7:
time: 149 us
  Pallas kernels  148 us (99%)
    pallas_call x1, Pallas kernels, on_device(): pl.pallas_call(kernel, out_shape=(jax.ShapeDtypeStruct((128, 2048), BF16)...  143 us
    pallas_call x1, Pallas kernels, on_device(): pl.pallas_call(finish, out_shape=[jax.ShapeDtypeStruct(p.shape, kind) for...  5.36 us

profile of v7, /device:TPU:1, one launch (start us, length us, event | category | flops | bytes accessed | tf_op | source)
XLA Modules:
  0.0 148.6 jit_solution(8256340027903818725)
XLA Ops:
  0.6 142.6 %group_attention.1 = (bf16[128,2048]{1,0:T(8,128)(2,1)}, bf16[128,4096]{1,0:T(8,128)(2,1)}, f32[512,128]{1,0:T(8,128)}, bf16[4,128,2048]{2,1,0:T(8,128)(2,1)}, bf16[4,128,2048]{2,1,0:T(8,128)(2,1)}) custom-call(bf16[128,4096]{1,0:T(8,128)(2,1)} %hidden.1, bf16[256,2048]{1,0:T(8,128)(2,1)} %weight.1, bf16[4,128,2048]{2,1,0:T(8,128)(2,1)} %keys.1, ...), custom_call_target="tpu_custom_call" | custom-call | tf_op jit(solution)/shard_map/group_attention/pallas_call | solution.py:658
  143.2 5.4 %finish.1 = (bf16[128,2048]{1,0:T(8,128)(2,1)}, bf16[128,4096]{1,0:T(8,128)(2,1)}, f32[512,128]{1,0:T(8,128)}, f32[512,2048]{1,0:T(8,128)}, f32[512,2048]{1,0:T(8,128)}) custom-call(bf16[128,2048]{1,0:T(8,128)(2,1)} %get-tuple-element.15.att_in, bf16[128,4096]{1,0:T(8,128)(2,1)} %get-tuple-element.16.dh_in, f32[512,128]{1,0:T(8,128)} %get-tuple-element.17.dwq_in, ...), custom_call_target="tpu_custom_call" | custom-call | tf_op jit(solution)/shard_map/finish/pallas_call | solution.py:709
